TPU v7x, 32 devices: a whole 2x2x4 slice. The times are simulated.
32 devices in a mesh: dp: 8 (over z, y), tensor: 4 (over x, core).
Axes of the slice: x: 2, y: 2, z: 4, core: 2. Of those that a mesh axis runs over, the one named last changes fastest.
Arguments:
- inputs: bfloat16 [16384, 768], P('dp'), may hold values from -6 to 6
- segments: int32 [64, 256], P('dp'), may hold values from 0 to 3, never falling along the last dimension, each value on 1 to 128 neighbouring positions
- query_weight: bfloat16 [768, 768], P('dp', 'tensor'), may hold values from -0.21875 to 0.21875
- key_weight: bfloat16 [768, 768], P('dp', 'tensor'), may hold values from -0.21875 to 0.21875
- value_weight: bfloat16 [768, 768], P('dp', 'tensor'), may hold values from -0.21875 to 0.21875
- query_bias: float32 [768], P('tensor'), may hold values from -3 to 3
- value_bias: float32 [768], P('tensor'), may hold values from -3 to 3
- out_weight: bfloat16 [768, 768], P('tensor', 'dp'), may hold values from -1.75 to 1.75
- out_bias: float32 [768], replicated, may hold values from -3 to 3
- first_gain: float32 [768], replicated, may hold values from 0.5 to 1.5
- first_shift: float32 [768], replicated, may hold values from -2 to 2
- inner_weight: bfloat16 [768, 3072], P('dp', 'tensor'), may hold values from -0.21875 to 0.21875
- inner_bias: float32 [3072], P('tensor'), may hold values from -3 to 3
- outer_weight: bfloat16 [3072, 768], P('tensor', 'dp'), may hold values from -0.109375 to 0.109375
- outer_bias: float32 [768], replicated, may hold values from -3 to 3
- second_gain: float32 [768], replicated, may hold values from 0.5 to 1.5
- second_shift: float32 [768], replicated, may hold values from -2 to 2
- cotangent: bfloat16 [16384, 768], P('dp'), may hold values from -6 to 6
Outputs:
- layer_out: bfloat16 [16384, 768], P('dp')
- input_grad: float32 [16384, 768], P('dp')
- query_weight_grad: float32 [768, 768], P('dp', 'tensor')
- key_weight_grad: float32 [768, 768], P('dp', 'tensor')
- value_weight_grad: float32 [768, 768], P('dp', 'tensor')
- query_bias_grad: float32 [768], P('tensor')
- value_bias_grad: float32 [768], P('tensor')
- out_weight_grad: float32 [768, 768], P('tensor', 'dp')
- out_bias_grad: float32 [768], replicated
- first_gain_grad: float32 [768], replicated
- first_shift_grad: float32 [768], replicated
- inner_weight_grad: float32 [768, 3072], P('dp', 'tensor')
- inner_bias_grad: float32 [3072], P('tensor')
- outer_weight_grad: float32 [3072, 768], P('tensor', 'dp')
- outer_bias_grad: float32 [768], replicated
- second_gain_grad: float32 [768], replicated
- second_shift_grad: float32 [768], replicated
Inputs may be any that keep to these rules, and one draw needn't show every extreme that they name: `segments`: in each packed sequence the segment numbers never fall; each segment holds 1 to 128 rows and one holds exactly 128.
All inputs are finite; a program needn't handle non-finite values.
Results may differ from a plain program's by a relative error of at most 0.019.
Values may be sent and summed in bfloat16 or wider, within the bound.
No kernel may reach another device: no remote copies, remote signals or barrier semaphores. Data moves between devices by JAX's collectives and lax.ppermute only.
A program may use at most 192 MiB of HBM per device.

v0:
```python
import jax
import jax.numpy as jnp
from jax import lax
from jax.sharding import PartitionSpec as P

HEAD_DIM = 64
LEN = 256
BLOCK_SEQS = 2


EPS = 1e-06


def matmul(left, right):
    return jnp.dot(left, right, preferred_element_type=jnp.float32)


def matmul_left(left, right):
    return lax.dot_general(
        left, right, (((0,), (0,)), ((), ())), preferred_element_type=jnp.float32
    )


def matmul_right(left, right):
    return lax.dot_general(
        left, right, (((1,), (1,)), ((), ())), preferred_element_type=jnp.float32
    )


def norm_forward(hidden, gain, shift):
    center = hidden - jnp.mean(hidden, axis=-1, keepdims=True)
    scale = lax.rsqrt(jnp.mean(center * center, axis=-1, keepdims=True) + EPS)
    normed = center * scale
    return (normed * gain + shift, normed, scale)


def norm_backward(incoming, normed, scale, gain):
    scaled = incoming * gain
    inner = (
        scaled
        - jnp.mean(scaled, axis=-1, keepdims=True)
        - normed * jnp.mean(scaled * normed, axis=-1, keepdims=True)
    )
    return (inner * scale, jnp.sum(incoming * normed, axis=0), jnp.sum(incoming, axis=0))


def masked_scores(query, key, seg_block):
    scores = jnp.einsum(
        "sqhd,skhd->shqk", query, key, preferred_element_type=jnp.float32
    ) * HEAD_DIM ** (-0.5)
    keep = seg_block[:, :, None] == seg_block[:, None, :]
    return jnp.where(keep[:, None], scores, -1e30)


def attend_forward(item):
    query, key, value, seg_block = item
    scores = masked_scores(query, key, seg_block)
    top = jnp.max(scores, axis=-1, keepdims=True)
    expo = jnp.exp(scores - top)
    total = jnp.sum(expo, axis=-1, keepdims=True)
    probs = (expo / total).astype(jnp.bfloat16)
    context = jnp.einsum("shqk,skhd->sqhd", probs, value, preferred_element_type=jnp.float32)
    return (context.astype(jnp.bfloat16), (top + jnp.log(total))[..., 0])


def attend_backward(item):
    query, key, value, seg_block, logsum, grad_context = item
    scores = masked_scores(query, key, seg_block)
    probs = jnp.exp(scores - logsum[..., None])
    grad_value = jnp.einsum(
        "shqk,sqhd->skhd",
        probs.astype(jnp.bfloat16),
        grad_context,
        preferred_element_type=jnp.float32,
    )
    grad_probs = jnp.einsum(
        "sqhd,skhd->shqk", grad_context, value, preferred_element_type=jnp.float32
    )
    delta = jnp.sum(grad_probs * probs, axis=-1, keepdims=True)
    grad_scores = (probs * (grad_probs - delta)).astype(jnp.bfloat16)
    factor = HEAD_DIM ** (-0.5)
    grad_query = (
        jnp.einsum("shqk,skhd->sqhd", grad_scores, key, preferred_element_type=jnp.float32) * factor
    )
    grad_key = (
        jnp.einsum("shqk,sqhd->skhd", grad_scores, query, preferred_element_type=jnp.float32)
        * factor
    )
    return (
        grad_query.astype(jnp.bfloat16),
        grad_key.astype(jnp.bfloat16),
        grad_value.astype(jnp.bfloat16),
    )


def exact_gelu(values):
    return jax.nn.gelu(values, approximate=False)


def body(
    inputs,
    segments,
    query_weight,
    key_weight,
    value_weight,
    query_bias,
    value_bias,
    out_weight,
    out_bias,
    first_gain,
    first_shift,
    inner_weight,
    inner_bias,
    outer_weight,
    outer_bias,
    second_gain,
    second_shift,
    cotangent,
):
    rows = inputs.shape[0]
    query_full, key_full, value_full, out_full, inner_full, outer_full = (
        lax.all_gather(query_weight, "dp", axis=0, tiled=True),
        lax.all_gather(key_weight, "dp", axis=0, tiled=True),
        lax.all_gather(value_weight, "dp", axis=0, tiled=True),
        lax.all_gather(out_weight, "dp", axis=1, tiled=True),
        lax.all_gather(inner_weight, "dp", axis=0, tiled=True),
        lax.all_gather(outer_weight, "dp", axis=1, tiled=True),
    )
    local = query_full.shape[1]
    heads = local // HEAD_DIM
    block = BLOCK_SEQS * LEN
    count = rows // block
    split = (count, BLOCK_SEQS, LEN, heads, HEAD_DIM)
    query = (matmul(inputs, query_full) + query_bias).astype(jnp.bfloat16)
    key = matmul(inputs, key_full).astype(jnp.bfloat16)
    value = (matmul(inputs, value_full) + value_bias).astype(jnp.bfloat16)
    query_blocks = query.reshape(split)
    key_blocks = key.reshape(split)
    value_blocks = value.reshape(split)
    seg_blocks = segments.reshape(count, BLOCK_SEQS, LEN)
    context, logsum = lax.map(attend_forward, (query_blocks, key_blocks, value_blocks, seg_blocks))
    context = context.reshape(rows, local)
    attn_sum = lax.psum(matmul(context, out_full).astype(jnp.bfloat16), "tensor").astype(
        jnp.float32
    )
    first_out, first_normed, first_scale = norm_forward(
        attn_sum + out_bias + inputs.astype(jnp.float32), first_gain, first_shift
    )
    first_low = first_out.astype(jnp.bfloat16)
    inner = matmul(first_low, inner_full) + inner_bias
    active_full, gelu_pull = jax.vjp(exact_gelu, inner)
    active = active_full.astype(jnp.bfloat16)
    ffn_sum = lax.psum(matmul(active, outer_full).astype(jnp.bfloat16), "tensor").astype(
        jnp.float32
    )
    out_value, second_normed, second_scale = norm_forward(
        ffn_sum + outer_bias + first_out, second_gain, second_shift
    )
    layer_out = out_value.astype(jnp.bfloat16)
    grad_second, second_gain_grad, second_shift_grad = norm_backward(
        cotangent.astype(jnp.float32), second_normed, second_scale, second_gain
    )
    outer_bias_grad = jnp.sum(grad_second, axis=0)
    grad_ffn = grad_second.astype(jnp.bfloat16)
    outer_local = matmul_left(active, grad_ffn)
    grad_inner = gelu_pull(matmul_right(grad_ffn, outer_full))[0].astype(jnp.bfloat16)
    inner_bias_grad = jnp.sum(grad_inner, axis=0, dtype=jnp.float32)
    inner_local = matmul_left(first_low, grad_inner)
    grad_first = (
        lax.psum(matmul_right(grad_inner, inner_full).astype(jnp.bfloat16), "tensor").astype(
            jnp.float32
        )
        + grad_second
    )
    grad_attn_in, first_gain_grad, first_shift_grad = norm_backward(
        grad_first, first_normed, first_scale, first_gain
    )
    out_bias_grad = jnp.sum(grad_attn_in, axis=0)
    grad_attn = grad_attn_in.astype(jnp.bfloat16)
    out_local = matmul_left(context, grad_attn)
    grad_context = matmul_right(grad_attn, out_full).astype(jnp.bfloat16)
    grad_query, grad_key, grad_value = lax.map(
        attend_backward,
        (query_blocks, key_blocks, value_blocks, seg_blocks, logsum, grad_context.reshape(split)),
    )
    grad_query = grad_query.reshape(rows, local)
    grad_key = grad_key.reshape(rows, local)
    grad_value = grad_value.reshape(rows, local)
    query_bias_grad = jnp.sum(grad_query, axis=0, dtype=jnp.float32)
    value_bias_grad = jnp.sum(grad_value, axis=0, dtype=jnp.float32)
    query_local = matmul_left(inputs, grad_query)
    key_local = matmul_left(inputs, grad_key)
    value_local = matmul_left(inputs, grad_value)
    input_part = (
        matmul_right(grad_query, query_full)
        + matmul_right(grad_key, key_full)
        + matmul_right(grad_value, value_full)
    )
    input_grad = (
        lax.psum(input_part.astype(jnp.bfloat16), "tensor").astype(jnp.float32) + grad_attn_in
    )
    (
        query_weight_grad,
        key_weight_grad,
        value_weight_grad,
        out_weight_grad,
        inner_weight_grad,
        outer_weight_grad,
    ) = (
        lax.psum_scatter(query_local, "dp", scatter_dimension=0, tiled=True),
        lax.psum_scatter(key_local, "dp", scatter_dimension=0, tiled=True),
        lax.psum_scatter(value_local, "dp", scatter_dimension=0, tiled=True),
        lax.psum_scatter(out_local, "dp", scatter_dimension=1, tiled=True),
        lax.psum_scatter(inner_local, "dp", scatter_dimension=0, tiled=True),
        lax.psum_scatter(outer_local, "dp", scatter_dimension=1, tiled=True),
    )
    (
        query_bias_grad,
        value_bias_grad,
        out_bias_grad,
        first_gain_grad,
        first_shift_grad,
        inner_bias_grad,
        outer_bias_grad,
        second_gain_grad,
        second_shift_grad,
    ) = lax.psum(
        (
            query_bias_grad,
            value_bias_grad,
            out_bias_grad,
            first_gain_grad,
            first_shift_grad,
            inner_bias_grad,
            outer_bias_grad,
            second_gain_grad,
            second_shift_grad,
        ),
        "dp",
    )
    return (
        layer_out,
        input_grad,
        query_weight_grad,
        key_weight_grad,
        value_weight_grad,
        query_bias_grad,
        value_bias_grad,
        out_weight_grad,
        out_bias_grad,
        first_gain_grad,
        first_shift_grad,
        inner_weight_grad,
        inner_bias_grad,
        outer_weight_grad,
        outer_bias_grad,
        second_gain_grad,
        second_shift_grad,
    )


def solution(mesh):
    in_specs = (
        P("dp", None),
        P("dp", None),
        P("dp", "tensor"),
        P("dp", "tensor"),
        P("dp", "tensor"),
        P("tensor"),
        P("tensor"),
        P("tensor", "dp"),
        P(),
        P(),
        P(),
        P("dp", "tensor"),
        P("tensor"),
        P("tensor", "dp"),
        P(),
        P(),
        P(),
        P("dp", None),
    )
    out_specs = (
        P("dp", None),
        P("dp", None),
        P("dp", "tensor"),
        P("dp", "tensor"),
        P("dp", "tensor"),
        P("tensor"),
        P("tensor"),
        P("tensor", "dp"),
        P(),
        P(),
        P(),
        P("dp", "tensor"),
        P("tensor"),
        P("tensor", "dp"),
        P(),
        P(),
        P(),
    )
    return jax.shard_map(body, mesh=mesh, in_specs=in_specs, out_specs=out_specs, check_vma=False)
```

profile of v0, /device:TPU:0, one launch (start us, length us, event | category | flops | bytes accessed | tf_op | source)
XLA Modules:
  0.0 945.9 jit_solution(3520162648662861878)
XLA Ops:
  8.1 33.1 %all_gather.18 = bf16[768,192]{1,0:T(8,128)(2,1)S(1)} all-gather(bf16[96,192]{1,0:T(8,128)(2,1)} %param.26), channel_id=1, replica_groups=mesh['dp'=8,'tensor'=4] {'dp'}, dimensions={0}, use_global_device_ids=true | all-gather | bytes 331776 | tf_op jit(solution)/shard_map/all_gather | solution.py:124
  42.0 4.0 fusion.49
  46.0 3.2 reshape.148
  49.2 2.2 copy.71
  51.4 31.1 %all_gather.19 = bf16[768,192]{1,0:T(8,128)(2,1)S(1)} all-gather(bf16[96,192]{1,0:T(8,128)(2,1)S(1)} %copy-done.19), channel_id=1, replica_groups=mesh['dp'=8,'tensor'=4] {'dp'}, dimensions={0}, use_global_device_ids=true | all-gather | bytes 331776 | tf_op jit(solution)/shard_map/all_gather | solution.py:122
  83.2 2.1 fusion.50
  85.3 3.3 reshape.150
  88.6 2.2 copy.72
  90.7 31.2 %all_gather.20 = bf16[768,192]{1,0:T(8,128)(2,1)S(1)} all-gather(bf16[96,192]{1,0:T(8,128)(2,1)} %param.25), channel_id=1, replica_groups=mesh['dp'=8,'tensor'=4] {'dp'}, dimensions={0}, use_global_device_ids=true | all-gather | bytes 331776 | tf_op jit(solution)/shard_map/all_gather | solution.py:123
  121.9 2.1 convolution_convert_fusion.6
  124.0 3.2 reshape.151
  127.2 2.2 copy.73
  130.7 18.8 %while.26 = (s32[]{:T(128)}, bf16[4,2,256,3,64]{2,1,0,4,3:T(2,128)(2,1)}, f32[4,2,3,256]{3,2,1,0:T(4,128)}, bf16[4,2,256,3,64]{2,4,3,1,0:T(8,128)(2,1)}, s32[4,2...) while((s32[]{:T(128)}, ...), condition=%wide.region_3.4_spmd, body=%wide.region_0.3_spmd.sunk | while | flops 104036864 | bytes 6220377 | solution.py:141
  149.6 3.2 reshape.152
  154.2 31.4 %all_gather.21 = bf16[192,768]{0,1:T(8,128)(2,1)S(1)} all-gather(bf16[192,96]{0,1:T(8,128)(2,1)} %copy.75), channel_id=1, replica_groups=mesh['dp'=8,'tensor'=4] {'dp'}, dimensions={1}, use_global_device_ids=true | all-gather | bytes 331776 | tf_op jit(solution)/shard_map/all_gather | solution.py:125
  186.4 3.9 convolution_convert_fusion.4
  191.5 68.4 %all-reduce.6.cloned.1.call-done = bf16[2048,768]{1,0:T(8,128)(2,1)} async-done(((bf16[2048,768]{1,0:T(8,128)(2,1)}), bf16[2048,768]{1,0:T(8,128)(2,1)}) %all-reduce.6.cloned.1.call-update) | async-done | bytes 3145744 | tf_op jit(solution)/shard_map/psum | solution.py:143
  259.9 3.3 fusion.48
  263.2 1.8 multiply_reduce_fusion.4
  265.0 20.1 %multiply_convert_fusion.1 = (bf16[2048,768]{1,0:T(8,128)(2,1)}, f32[2048,768]{1,0:T(8,128)}, f32[2048,768]{1,0:T(8,128)}) fusion(f32[768]{0:T(1024)} %param.34, bf16[768,768]{1,0:T(8,128)(2,1)} %all-gather.3.cloned.1.call-done, f32[768]{0:T(1024)} %param.32, f32[768]{0:T(1024)} %param.31, f32[2048]{0:T(1024)S(1)} %add_rsqrt_fusion.1, ...), kind=kOutput, calls=%fused_computation.77 | convolution fusion | flops 2533883904 | bytes 23228416 | tf_op jit(solution)/shard_map/dot_general | solution.py:15
  285.1 6.5 convolution_convert_fusion.3
  292.2 68.1 %all-reduce.8.cloned.1.call-done = bf16[2048,768]{1,0:T(8,128)(2,1)} async-done(((bf16[2048,768]{1,0:T(8,128)(2,1)}), bf16[2048,768]{1,0:T(8,128)(2,1)}) %all-reduce.8.cloned.1.call-update) | async-done | bytes 3145744 | tf_op jit(solution)/shard_map/psum | solution.py:153
  360.3 4.7 fusion.69
  366.9 3.6 fusion.41
  370.5 4.0 fusion.38
  374.5 9.4 convert_reduce_fusion.1
  383.9 1.7 copy-done.37
  385.6 4.0 convolution_convert_fusion.2
  389.9 68.5 %all-reduce.10.cloned.1.call-done = bf16[2048,768]{1,0:T(8,128)(2,1)} async-done(((bf16[2048,768]{1,0:T(8,128)(2,1)}), bf16[2048,768]{1,0:T(8,128)(2,1)}) %all-reduce.10.cloned.1.call-update) | async-done | bytes 3145744 | tf_op jit(solution)/shard_map/psum | solution.py:170
  458.3 9.4 multiply_reduce_fusion.1
  467.8 6.3 fusion.68
  474.1 2.6 convolution_convert_fusion.5
  477.0 2.3 fusion.60
  479.4 3.3 reshape.153
  483.9 43.9 %while.27 = (s32[]{:T(128)}, bf16[4,2,256,3,64]{2,4,3,1,0:T(8,128)(2,1)}, bf16[4,2,256,3,64]{2,1,0,4,3:T(2,128)(2,1)}, bf16[4,2,256,3,64]{2,4,3,1,0:T(8,128)(2,1...) while((s32[]{:T(128)}, ...), condition=%wide.region_17.18_spmd, body=%wide.region_15.17_spmd.sunk | while | flops 255818240 | bytes 14852217 | solution.py:182
  485.5 1.6 subtract_exponential_fusion.3
  492.0 1.9 fusion.133
  503.0 1.9 fusion.133
  514.0 1.9 fusion.133
  524.9 1.9 fusion.133
  527.8 2.8 copy.80
  530.7 3.1 reshape.154
  534.1 5.0 fusion.72
  539.0 3.2 reshape.155
  542.2 2.8 copy.82
  545.0 3.1 reshape.156
  548.2 2.3 fusion.73
  550.5 5.7 add_convert_fusion
  556.3 2.7 convolution_bitcast_fusion.2
  559.0 2.2 copy.90
  561.4 2.9 convolution_bitcast_fusion
  564.2 2.2 copy.94
  566.5 2.7 convolution_bitcast_fusion.1
  569.3 2.2 copy.92
  571.9 7.7 fusion.63
  579.7 7.9 fusion.54
  589.4 38.0 %all-reduce = (f32[192]{0:T(256)}, f32[192]{0:T(256)}, f32[768]{0:T(1024)}, f32[768]{0:T(1024)}, f32[768]{0:T(1024)}, /*index=5*/f32[768]{0:T(1024)}, f32[768]{0:T(1024)}, f32[768]{0:T(1024)}, f32[768]{0:T(1024)}) all-reduce(f32[192]{0:T(256)S(1)} %reduce_sum.184, ...), channel_id=1, replica_groups=mesh['dp'=8,'tensor'=4] {'dp'}, use_global_device_ids=true, to_apply=%region_23.24 | all-reduce | flops 5760 | bytes 46080 | tf_op jit(solution)/shard_map/psum | solution.py:227
  627.5 1.6 copy.97
  629.1 7.1 convert_add_fusion
  636.1 26.5 %reduce-scatter.19.cloned.1.call-done = f32[96,192]{1,0:T(8,128)} async-done(((f32[768,192]{1,0:T(8,128)}), f32[96,192]{1,0:T(8,128)}) %reduce-scatter.19.cloned.1.call-update) | async-done | bytes 73744
  662.7 65.5 %reduce-scatter.23.cloned.1.call-done = f32[96,192]{1,0:T(8,128)} async-done(((f32[768,192]{1,0:T(8,128)}), f32[96,192]{1,0:T(8,128)}) %reduce-scatter.23.cloned.1.call-update) | async-done | bytes 73744
  728.2 65.9 %reduce-scatter.21.cloned.1.call-done = f32[96,192]{1,0:T(8,128)} async-done(((f32[768,192]{1,0:T(8,128)}), f32[96,192]{1,0:T(8,128)}) %reduce-scatter.21.cloned.1.call-update) | async-done | bytes 73744
  794.1 72.2 %reduce-scatter.15.cloned.1.call-done = f32[96,768]{1,0:T(8,128)} async-done(((f32[768,768]{1,0:T(8,128)}), f32[96,768]{1,0:T(8,128)}) %reduce-scatter.15.cloned.1.call-update) | async-done | bytes 294928 | tf_op jit(solution)/shard_map/reduce_scatter | solution.py:214
  866.2 72.2 %reduce-scatter.17.cloned.1.call-done = f32[768,96]{0,1:T(8,128)} async-done(((f32[768,768]{0,1:T(8,128)}), f32[768,96]{0,1:T(8,128)}) %reduce-scatter.17.cloned.1.call-update) | async-done | bytes 294928 | tf_op jit(solution)/shard_map/reduce_scatter | solution.py:215
  (194 shorter events, 66.8 us)
Async XLA Ops:
  8.0 75.2 %copy-start = (bf16[2048,768]{1,0:T(8,128)(2,1)S(1)}, bf16[2048,768]{1,0:T(8,128)(2,1)}, u32[]{:S(2)}) copy-start(bf16[2048,768]{1,0:T(8,128)(2,1)} %param.22) | copy-start | bytes 9437188
  8.0 43.4 %copy-start.19 = (bf16[96,192]{1,0:T(8,128)(2,1)S(1)}, bf16[96,192]{1,0:T(8,128)(2,1)}, u32[]{:S(2)}) copy-start(bf16[96,192]{1,0:T(8,128)(2,1)} %param.24) | copy-start | bytes 110596
  8.0 75.2 %copy-start.36 = (f32[192]{0:T(256)S(1)}, f32[192]{0:T(256)}, u32[]{:S(2)}) copy-start(f32[192]{0:T(256)} %param.27) | copy-start | bytes 2308
  8.1 251.8 %all-reduce.6.cloned.1.call-start = ((), (), s32[]{:S(2)}) async-start(), calls=%async_computation.6 | async-start | bytes 6291456 | tf_op jit(solution)/shard_map/psum | solution.py:143
  41.2 0.8 copy-start.13
  82.5 0.7 copy-start.12
  85.3 44.1 %copy-start.29 = (s32[8,256]{1,0:T(8,128)S(1)}, s32[8,256]{1,0:T(8,128)}, u32[]{:S(2)}) copy-start(s32[8,256]{1,0:T(8,128)} %param.23) | copy-start | bytes 24580
  149.5 110.3 %copy-start.18 = (s32[4,2,256]{2,1,0:T(2,128)}, s32[4,2,256]{2,1,0:T(2,128)S(1)}, u32[]{:S(2)}) copy-start(s32[4,2,256]{2,1,0:T(2,128)S(1)} %get-tuple-element.497) | copy-start | bytes 24580
  149.6 110.3 %copy-start.15 = (f32[768]{0:T(1024)S(1)}, f32[768]{0:T(1024)}, u32[]{:S(2)}) copy-start(f32[768]{0:T(1024)} %param.30) | copy-start | bytes 9220
  185.6 0.8 copy-start.9
  190.3 74.7 %all-gather.3.cloned.1.call-start = ((), (), s32[]{:S(2)}) async-start(), calls=%async_computation.7 | async-start | bytes 1327104 | tf_op jit(solution)/shard_map/all_gather | solution.py:126
  190.9 94.3 %all-gather.5.cloned.1.call-start = ((), (), s32[]{:S(2)}) async-start(), calls=%async_computation.8 | async-start | bytes 1327104 | tf_op jit(solution)/shard_map/all_gather | solution.py:127
  191.5 168.8 %all-reduce.8.cloned.1.call-start = ((), (), s32[]{:S(2)}) async-start(), calls=%async_computation.9 | async-start | bytes 6291456 | tf_op jit(solution)/shard_map/psum | solution.py:153
  259.9 3.3 copy-start.2
  291.7 166.6 %all-reduce.10.cloned.1.call-start = ((), (), s32[]{:S(2)}) async-start(), calls=%async_computation.10 | async-start | bytes 6291456 | tf_op jit(solution)/shard_map/psum | solution.py:170
  365.0 1.9 copy-start.5
  365.0 1.9 copy-start.22
  365.9 4.6 copy-start.30
  366.9 7.6 slice-start
  370.5 4.0 copy-start.34
  370.5 4.0 copy-start.35
  370.5 4.0 slice-start.1
  374.5 9.4 copy-start.4
  374.5 11.1 %copy-start.33 = (bf16[768,768]{1,0:T(8,128)(2,1)S(1)}, bf16[768,768]{1,0:T(8,128)(2,1)}, u32[]{:S(2)}) copy-start(bf16[768,768]{1,0:T(8,128)(2,1)} %all-gather.3.cloned.1.call-done) | copy-start | bytes 3538948
  383.9 1.7 copy-start.37
  389.6 237.8 %reduce-scatter.25.cloned.1.call-start = ((), (), s32[]{:S(2)}) async-start(), calls=%async_computation.17 | async-start | bytes 884736
  458.3 9.4 copy-start.3
  458.3 9.4 copy-start.6
  458.3 9.4 copy-start.16
  458.3 9.4 copy-start.20
  467.8 6.3 copy-start.10
  474.1 2.9 copy-start.1
  474.1 2.9 copy-start.8
  533.8 95.3 %all-reduce.12.cloned.1.call-start = ((), (), s32[]{:S(2)}) async-start(), calls=%async_computation.11 | async-start | bytes 6291456 | tf_op jit(solution)/shard_map/psum | solution.py:200
  548.2 2.3 copy-start.7
  548.2 2.3 copy-start.14
  556.3 106.4 %reduce-scatter.19.cloned.1.call-start = ((), (), s32[]{:S(2)}) async-start(), calls=%async_computation.14 | async-start | bytes 884736
  561.3 10.6 %copy-start.17 = (f32[768]{0:T(1024)S(1)}, f32[768]{0:T(1024)}, u32[]{:S(2)}) copy-start(f32[768]{0:T(1024)} %param.30) | copy-start | bytes 9220
  561.3 10.6 %copy-start.21 = (f32[768]{0:T(1024)S(1)}, f32[768]{0:T(1024)}, u32[]{:S(2)}) copy-start(f32[768]{0:T(1024)} %param.31) | copy-start | bytes 9220
  561.3 10.5 %copy-start.31 = (f32[768]{0:T(1024)S(1)}, f32[768]{0:T(1024)}, u32[]{:S(2)}) copy-start(f32[768]{0:T(1024)} %param.32) | copy-start | bytes 9220
  561.3 166.9 %reduce-scatter.23.cloned.1.call-start = ((), (), s32[]{:S(2)}) async-start(), calls=%async_computation.16 | async-start | bytes 884736
  566.5 227.6 %reduce-scatter.21.cloned.1.call-start = ((), (), s32[]{:S(2)}) async-start(), calls=%async_computation.15 | async-start | bytes 884736
  571.5 294.7 %reduce-scatter.15.cloned.1.call-start = ((), (), s32[]{:S(2)}) async-start(), calls=%async_computation.12 | async-start | bytes 2654208 | tf_op jit(solution)/shard_map/reduce_scatter | solution.py:214
  579.6 8.1 copy-start.11
  579.6 9.8 %copy-start.23 = (f32[768]{0:T(1024)S(1)}, f32[768]{0:T(1024)}, u32[]{:S(2)}) copy-start(f32[768]{0:T(1024)} %get-tuple-element.218) | copy-start | bytes 9220
  579.6 9.8 %copy-start.24 = (f32[768]{0:T(1024)S(1)}, f32[768]{0:T(1024)}, u32[]{:S(2)}) copy-start(f32[768]{0:T(1024)} %get-tuple-element.224) | copy-start | bytes 9220
  579.6 9.8 %copy-start.25 = (f32[768]{0:T(1024)S(1)}, f32[768]{0:T(1024)}, u32[]{:S(2)}) copy-start(f32[768]{0:T(1024)} %get-tuple-element.216) | copy-start | bytes 9220
  579.6 9.8 %copy-start.26 = (f32[768]{0:T(1024)S(1)}, f32[768]{0:T(1024)}, u32[]{:S(2)}) copy-start(f32[768]{0:T(1024)} %get-tuple-element.221) | copy-start | bytes 9220
  579.7 9.8 %copy-start.27 = (f32[768]{0:T(1024)S(1)}, f32[768]{0:T(1024)}, u32[]{:S(2)}) copy-start(f32[768]{0:T(1024)} %get-tuple-element.222) | copy-start | bytes 9220
  579.7 9.8 %copy-start.28 = (f32[768]{0:T(1024)S(1)}, f32[768]{0:T(1024)}, u32[]{:S(2)}) copy-start(f32[768]{0:T(1024)} %get-tuple-element.268) | copy-start | bytes 9220
  579.7 9.8 %copy-start.32 = (f32[768]{0:T(1024)S(1)}, f32[768]{0:T(1024)}, u32[]{:S(2)}) copy-start(f32[768]{0:T(1024)} %get-tuple-element.281) | copy-start | bytes 9220
  579.7 358.7 %reduce-scatter.17.cloned.1.call-start = ((), (), s32[]{:S(2)}) async-start(), calls=%async_computation.13 | async-start | bytes 2654208 | tf_op jit(solution)/shard_map/reduce_scatter | solution.py:215
Sparse Core Ops, SparseCore 0:
  190.4 69.4 all-reduce.5
  291.8 68.4 all-reduce.7
  389.8 68.5 all-reduce.9
  556.4 68.6 all-reduce.11
Sparse Core Ops, SparseCore 1:
  192.9 42.4 all-gather.2
  237.4 39.8 all-gather.4
  533.9 62.7 reduce-scatter.24
  600.9 61.7 reduce-scatter.18
  666.6 61.6 reduce-scatter.22
  732.5 61.6 reduce-scatter.20
  798.0 68.2 reduce-scatter.14
  870.2 68.2 reduce-scatter.16
where the time goes:
time: 956 us; the launch traced here: 946 us
  waiting for transfers between devices  508 us (53%)
  blocking collectives  165 us (17%)
  matrix products  134 us (14%)
  local copies, waits for them, and re-layouts  73 us (8%)
  other arithmetic  48.2 us (5%)
  between operations  16.2 us (2%)
    unnamed x16, waiting for transfers between devices  159 us
    reduce_scatter x1, waiting for transfers between devices, body(): lax.psum_scatter(outer_local, 'dp', scatter_dimension=1, tiled=True)  72.2 us
    reduce_scatter x1, waiting for transfers between devices, body(): lax.psum_scatter(inner_local, 'dp', scatter_dimension=0, tiled=True)  72.2 us
    psum x1, waiting for transfers between devices, body(): lax.psum(matmul_right(grad_inner, inner_full).astype(jnp.bfloat16), 'tens...  68.5 us
    psum x1, waiting for transfers between devices, body(): lax.psum(matmul(context, out_full).astype(jnp.bfloat16), 'tensor')  68.4 us
    psum x1, waiting for transfers between devices, body(): lax.psum(matmul(active, outer_full).astype(jnp.bfloat16), 'tensor')  68.1 us
    dot_general x6, matrix products, matmul(): return jnp.dot(left, right, preferred_element_type=jnp.float32)  38.6 us
    psum x1, blocking collectives, body(): lax.psum((query_bias_grad, value_bias_grad, out_bias_grad, first_gain_gra...  38 us
  transfers between devices with their start and end apart: 12, of which 8 were waited for; matrix products, arithmetic and copies ran while one was open for 9% of the time, Pallas kernels for 0%

commit v1 on v0

v1 whole, which is shorter than its diff:
```python
import functools
import math

import jax
import jax.numpy as jnp
from jax import lax
from jax.experimental import pallas as pl
from jax.experimental.pallas import tpu as pltpu
from jax.sharding import PartitionSpec as P

HEAD_DIM = 64
LEN = 256
EPS = 1e-06
BF = jnp.bfloat16
F32 = jnp.float32
AXES = ("dp", "tensor")
MIB = 1 << 20


def dot(left, right):
    return lax.dot_general(left, right, (((1,), (0,)), ((), ())), preferred_element_type=F32)


def dot_t(left, right):
    return lax.dot_general(left, right, (((1,), (1,)), ((), ())), preferred_element_type=F32)


def t_dot(left, right):
    return lax.dot_general(left, right, (((0,), (0,)), ((), ())), preferred_element_type=F32)


def vmem():
    return pl.BlockSpec(memory_space=pltpu.VMEM)


def smem():
    return pl.BlockSpec(memory_space=pltpu.SMEM)


def anywhere():
    return pl.BlockSpec(memory_space=pl.ANY)


def call(body, ins, in_specs, outs, out_specs, scratch, limit, flops):
    return pl.pallas_call(
        body,
        out_shape=outs,
        in_specs=in_specs,
        out_specs=out_specs,
        scratch_shapes=scratch,
        compiler_params=pltpu.CompilerParams(vmem_limit_bytes=limit * MIB),
        cost_estimate=pl.CostEstimate(flops=1000, bytes_accessed=1000, transcendentals=0),
    )(*ins)


def shape(dims, dtype):
    return jax.ShapeDtypeStruct(dims, dtype)


class Plan:
    def __init__(self, mesh):
        self.ndp, self.nt = mesh.shape["dp"], mesh.shape["tensor"]
        self.pieces = self.nt == 4 and self.ndp in (4, 8, 16)
        self.nz = self.ndp // 2

    def pairs(self, move):
        found = []
        for d in range(self.ndp):
            for t in range(self.nt):
                z, y, x, c = move(d >> 1, d & 1, t >> 1, t & 1)
                found.append((d * self.nt + t, (z * 2 + y) * self.nt + x * 2 + c))
        return found

    def first(self):
        return self.pairs(lambda z, y, x, c: (z, y, x ^ 1, c) if c == 0 else (z, y ^ 1, x, c))

    def second(self):
        return self.pairs(lambda z, y, x, c: (z, y, x ^ 1, c) if c == 1 else (z, y ^ 1, x, c))

    def core(self):
        return self.pairs(lambda z, y, x, c: (z, y, x, c ^ 1))

    def along(self, j):
        return self.pairs(lambda z, y, x, c: (z ^ j, y, x, c))

    def tables(self):
        d, t = lax.axis_index("dp"), lax.axis_index("tensor")
        z, y, x, c = d >> 1, d & 1, t >> 1, t & 1
        s = jnp.arange(2)[:, None, None]
        r = jnp.arange(4)[None, :, None]
        j = jnp.arange(self.nz)[None, None, :]
        a, b = r & 1, r >> 1
        core = c ^ s
        dx, dy = jnp.where(core == 0, a, b), jnp.where(core == 0, b, a)
        where_t = jnp.broadcast_to((x ^ dx) * 2 + core, (2, 4, self.nz))
        where_d = jnp.broadcast_to((z ^ j) * 2 + (y ^ dy), (2, 4, self.nz))
        s = jnp.arange(2)[:, None, None]
        xx = jnp.arange(2)[None, :, None]
        dd = jnp.arange(self.ndp)[None, None, :]
        core = c ^ s
        dx, dy = xx ^ x, (dd & 1) ^ y
        a, b = jnp.where(core == 0, dx, dy), jnp.where(core == 0, dy, dx)
        slot = jnp.broadcast_to((b * 2 + a) * self.nz + ((dd >> 1) ^ z), (2, 2, self.ndp))
        gather = jnp.stack([where_t.reshape(-1), where_d.reshape(-1)]).astype(jnp.int32)
        scatter = slot.reshape(4, self.ndp).astype(jnp.int32)
        return gather, scatter

    def turn(self, values, pairs):
        return lax.ppermute(values, AXES, pairs)

    def near(self, shard):
        return jnp.stack([shard] + [self.turn(shard, self.along(j)) for j in range(1, self.nz)])

    def share(self, part):
        other = self.turn(part, self.pairs(lambda z, y, x, c: (z, y, x ^ 1, c)))
        return [part, other, self.turn(part, self.core()), self.turn(other, self.core())]

    def add_core(self, keep, got, which):
        return keep[which].astype(F32) + got[which].astype(F32)

    def scatter_a(self, keep, got):
        away = jnp.stack([self.add_core(keep, got, r).astype(BF) for r in (1, 3)])
        return away, lambda: self.turn(away, self.first())

    def scatter_b(self, keep, got, got_a):
        away = (self.add_core(keep, got, 2) + got_a[1].astype(F32)).astype(BF)
        return away, lambda: self.turn(away, self.second())

    def scatter_z(self, keep, got, got_a, got_b):
        left = self.add_core(keep, got, 0) + got_a[0].astype(F32) + got_b.astype(F32)
        low = left[1:].astype(BF)
        moved = [self.turn(low[j - 1], self.along(j)) for j in range(1, self.nz)]
        total = left[0]
        for piece in moved:
            total = total + piece.astype(F32)
        return total

    def total(self, values):
        for pairs in (self.core(), self.first(), self.second()):
            values = values + self.turn(values, pairs)
        moved = [self.turn(values, self.along(j)) for j in range(1, self.nz)]
        for piece in moved:
            values = values + piece
        return values


def load_weights(refs, where, full, sem):
    if len(refs) == 1:
        for t in range(full.shape[0]):
            pltpu.make_async_copy(refs[0].at[t], full.at[t], sem.at[t]).start()
        return
    nz, rows, _ = refs[0].shape
    for r, ref in enumerate(refs):
        for j in range(nz):
            t, d = where[0, r * nz + j], where[1, r * nz + j]
            spot = pl.ds(pl.multiple_of(d * rows, rows), rows)
            pltpu.make_async_copy(ref.at[j], full.at[t, spot], sem.at[t]).start()


def load(ref, held, sem):
    pltpu.make_async_copy(ref, held, sem).start()


def wait(held, sem):
    pltpu.make_async_copy(held, held, sem).wait()


def blocks(rows, block):
    def over(run):
        @pl.loop(0, rows // block)
        def _(i):
            run(pl.ds(pl.multiple_of(i * block, block), block))

    return over


def tie(value, *after):
    return lax.optimization_barrier((value, *after))[0]


def lane_masks(rows):
    lane = lax.broadcasted_iota(jnp.int32, (rows, 128), 1)
    return lane < HEAD_DIM


def pick(mask, values):
    return jnp.where(mask, values, jnp.zeros_like(values))


def norm_stats(hidden):
    center = hidden - jnp.mean(hidden, axis=-1, keepdims=True)
    scale = lax.rsqrt(jnp.mean(center * center, axis=-1, keepdims=True) + EPS)
    return center * scale, scale


def norm_pull(incoming, normed, scale, gain):
    scaled = incoming * gain
    return scale * (
        scaled
        - jnp.mean(scaled, axis=-1, keepdims=True)
        - normed * jnp.mean(scaled * normed, axis=-1, keepdims=True)
    )


def attend_kernel(nw, x_ref, seg_row, seg_col, bias, out_bias, gain, shift, where, *rest):
    refs, rest = rest[:nw], rest[nw:]
    acts, probs, ctx, normed_ref, scale_ref, low_ref, full, keep, sem = rest
    rows = x_ref.shape[0]
    nt = acts.shape[0]
    load_weights(refs, where, full, sem)
    nseq = rows // LEN
    for s in range(nseq):
        same = seg_col[s * LEN : (s + 1) * LEN, :] == seg_row[s : s + 1, :]
        keep[s] = jnp.where(same, 0.0, -1e30).astype(F32)
    low_half = lane_masks(LEN)
    ones = jnp.ones((LEN, 128), BF)

    normed_ref[...] = x_ref[...].astype(F32) + out_bias[...]

    @pl.loop(0, nt)
    def _(t):
        wait(full.at[t], sem.at[t])
        x = x_ref[...]
        acts[t, :, 0:512] = (dot(x, full[t, :, 0:512]) + bias[t, :, 0:512]).astype(BF)
        last = dot(x, full[t, :, 512:640]).astype(BF)
        acts[t, :, 512:640] = pick(lane_masks(rows), last)

        for s in range(nseq):
            span = slice(s * LEN, (s + 1) * LEN)
            q01, k01, v01 = acts[t, span, 0:128], acts[t, span, 128:256], acts[t, span, 256:384]
            qv2, k2 = acts[t, span, 384:512], acts[t, span, 512:640]
            heads = (
                (pick(low_half, q01), k01, v01),
                (pick(~low_half, q01), k01, v01),
                (pick(low_half, qv2), k2, qv2),
            )
            done = []
            for h, (query, key, value) in enumerate(heads):
                scores = dot_t(query, key) * HEAD_DIM ** (-0.5) + keep[s]
                top = jnp.max(scores, axis=-1, keepdims=True)
                expo = jnp.exp(scores - top)
                low = expo.astype(BF)
                mixed = dot(low, jnp.concatenate([value, ones], axis=1))
                inverse = 1.0 / mixed[:, 128:]
                probs[t, s, h] = (expo * jnp.concatenate([inverse, inverse], axis=1)).astype(BF)
                done.append(mixed[:, :128] * inverse)
            ctx[t, span, 0:128] = pick(~low_half, done[2]).astype(BF)
            ctx[t, span, 128:256] = jnp.where(low_half, done[0], done[1]).astype(BF)
        part = dot_t(ctx[t], full[t, :, 512:768]).astype(BF)
        normed_ref[...] += part.astype(F32)

    @blocks(rows, 128)
    def _(span):
        normed, scale = norm_stats(normed_ref[span, :])
        normed_ref[span, :] = normed
        scale_ref[span, :] = jnp.broadcast_to(scale, (128, 128))
        low_ref[span, :] = (normed * gain[...] + shift[...]).astype(BF)


def erfc_parts(values):
    size = jnp.abs(values) * (1.0 / math.sqrt(2.0))
    t = 1.0 / (1.0 + 0.5 * size)
    poly = -0.82215223 + t * 0.17087277
    for c in (1.48851587, -1.13520398, 0.27886807, -0.18628806, 0.09678418, 0.37409196, 1.00002368):
        poly = c + t * poly
    bell = jnp.exp(-size * size)
    tail = 0.5 * t * jnp.exp(t * poly - 1.26551223) * bell
    return jnp.where(values >= 0, 1.0 - tail, tail), bell


def inner_kernel(nw, low_ref, bias, where, *rest):
    refs, rest = rest[:nw], rest[nw:]
    active, slope, full, inner_ref, sem = rest
    rows = low_ref.shape[0]
    nt = active.shape[0]
    load_weights(refs, where, full, sem)

    @pl.loop(0, nt)
    def _(t):
        wait(full.at[t], sem.at[t])
        inner_ref[...] = dot(low_ref[...], full[t]) + bias[t]

        @blocks(rows, 64)
        def _(span):
            inner = inner_ref[span, :]
            phi, bell = erfc_parts(inner)
            active[t, span, :] = (inner * phi).astype(BF)
            slope[t, span, :] = (phi + inner * bell * (1.0 / math.sqrt(2.0 * math.pi))).astype(BF)


def outer_kernel(nw, active, normed_ref, gain1, shift1, outer_bias, gain, shift, cot, where, *rest):
    refs, rest = rest[:nw], rest[nw:]
    out_ref, second_ref, ffn_ref, vec_ref, full, held, sem, sem_a = rest
    rows = normed_ref.shape[0]
    nt = active.shape[0]
    for t in range(nt):
        load(active.at[t], held.at[t], sem_a.at[t])
    load_weights(refs, where, full, sem)
    vec_ref[...] = jnp.zeros_like(vec_ref)
    second_ref[...] = normed_ref[...] * gain1[...] + shift1[...] + outer_bias[...]
    for t in range(nt):
        wait(held.at[t], sem_a.at[t])
        wait(full.at[t], sem.at[t])
        second_ref[...] += dot_t(held[t], full[t]).astype(BF).astype(F32)

    @blocks(rows, 128)
    def _(span):
        normed, scale = norm_stats(second_ref[span, :])
        out_ref[span, :] = (normed * gain[...] + shift[...]).astype(BF)
        incoming = cot[span, :].astype(F32)
        pulled = norm_pull(incoming, normed, scale, gain[...])
        second_ref[span, :] = pulled
        ffn_ref[span, :] = pulled.astype(BF)
        vec_ref[0:1, :] += jnp.sum(incoming * normed, axis=0, keepdims=True)
        vec_ref[1:2, :] += jnp.sum(incoming, axis=0, keepdims=True)
        vec_ref[2:3, :] += jnp.sum(pulled, axis=0, keepdims=True)


def store_grad(ndp, slots, line, held, out, sem):
    nz, rows = out.shape[1], out.shape[2]
    for d in range(ndp):
        slot = slots[line, d]
        pltpu.make_async_copy(held.at[pl.ds(d * rows, rows)], out.at[slot // nz, slot % nz], sem).start()


def grad_kernel(ndp, side, left, right, where, slots, out, part, held, sem_in, sem_out):
    core = (where[0, 0] % 2) ^ side
    for n in range(2):
        load(right.at[2 * n + core], part.at[n], sem_in.at[n])
    for n in range(2):
        wait(part.at[n], sem_in.at[n])
        held[n] = t_dot(left[...], part[n]).astype(BF)
        store_grad(ndp, slots, side * 2 + n, held.at[n], out, sem_out.at[n])
    for n in range(2):
        wait(held.at[n], sem_out.at[n])


def whole_grad_kernel(left, right, out):
    for t in range(out.shape[0]):
        out[t] = t_dot(left[...], right[t]).astype(BF)


def slope_kernel(nw, ffn_ref, slope, where, *rest):
    refs, rest = rest[:nw], rest[nw:]
    pulled, vec_ref, full, held, sem, sem_a = rest
    nt = slope.shape[0]
    load_weights(refs, where, full, sem)
    for t in range(nt):
        load(slope.at[t], held.at[t], sem_a.at[t])
    for t in range(nt):
        wait(full.at[t], sem.at[t])
        wait(held.at[t], sem_a.at[t])
        grad = (dot(ffn_ref[...], full[t]) * held[t].astype(F32)).astype(BF)
        pulled[t] = grad
        vec_ref[t] = jnp.sum(grad.astype(F32), axis=0, keepdims=True)


def first_kernel(nw, pulled, second, normed_ref, scale_ref, gain, where, *rest):
    inner_refs, refs, rest = rest[:nw], rest[nw : 2 * nw], rest[2 * nw :]
    attn_in, attn_low, ctx_grad, vec_ref, inner_full, full, held, sem_i, sem, sem_a = rest
    rows = second.shape[0]
    nt = pulled.shape[0]
    for t in range(nt):
        load(pulled.at[t], held.at[t], sem_a.at[t])
    load_weights(inner_refs, where, inner_full, sem_i)
    load_weights(refs, where, full, sem)
    vec_ref[...] = jnp.zeros_like(vec_ref)
    attn_in[...] = second[...]
    for t in range(nt):
        wait(held.at[t], sem_a.at[t])
        wait(inner_full.at[t], sem_i.at[t])
        attn_in[...] += dot_t(held[t], inner_full[t])

    @blocks(rows, 128)
    def _(span):
        incoming = attn_in[span, :]
        normed = normed_ref[span, :]
        grad = norm_pull(incoming, normed, scale_ref[span, 0:1], gain[...])
        attn_in[span, :] = grad
        attn_low[span, :] = grad.astype(BF)
        vec_ref[0:1, :] += jnp.sum(incoming * normed, axis=0, keepdims=True)
        vec_ref[1:2, :] += jnp.sum(incoming, axis=0, keepdims=True)
        vec_ref[2:3, :] += jnp.sum(grad, axis=0, keepdims=True)

    low_half = lane_masks(rows)
    for t in range(nt):
        wait(full.at[t], sem.at[t])
        got = dot(attn_low[...], full[t, :, 512:768])
        ctx_grad[t, :, 0:128] = pick(~low_half, got[:, :128]).astype(BF)
        ctx_grad[t, :, 128:256] = got[:, 128:].astype(BF)


def attend_pull_kernel(acts, probs, ctx_grad, back, vec_ref):
    nt, rows, _ = acts.shape
    nseq = rows // LEN
    low_half = lane_masks(LEN)
    factor = HEAD_DIM ** (-0.5)

    @pl.loop(0, nt)
    def _(t):
        for s in range(nseq):
            span = slice(s * LEN, (s + 1) * LEN)
            q01, k01, v01 = acts[t, span, 0:128], acts[t, span, 128:256], acts[t, span, 256:384]
            qv2, k2 = acts[t, span, 384:512], acts[t, span, 512:640]
            g2, g01 = ctx_grad[t, span, 0:128], ctx_grad[t, span, 128:256]
            heads = (
                (pick(low_half, g01), q01, k01, v01),
                (pick(~low_half, g01), q01, k01, v01),
                (g2, qv2, k2, qv2),
            )
            queries, keys, values = [], [], []
            for h, (grad, query, key, value) in enumerate(heads):
                prob = probs[t, s, h]
                wide = prob.astype(F32)
                pulled = dot_t(grad, value)
                delta = jnp.sum(pulled * wide, axis=-1, keepdims=True)
                scores = (wide * (pulled - delta)).astype(BF)
                queries.append(dot(scores, key) * factor)
                keys.append(t_dot(scores, query) * factor)
                values.append(t_dot(prob, grad))
            back[t, span, 0:128] = jnp.where(low_half, queries[0], queries[1]).astype(BF)
            back[t, span, 128:256] = jnp.where(low_half, keys[0], keys[1]).astype(BF)
            back[t, span, 256:384] = (values[0] + values[1]).astype(BF)
            back[t, span, 384:512] = jnp.where(low_half, queries[2], values[2]).astype(BF)
            back[t, span, 512:640] = pick(low_half, keys[2]).astype(BF)
        vec_ref[t] = jnp.sum(back[t].astype(F32), axis=0, keepdims=True)


def attn_grad_of(x_ref, attn_low, back, ctx):
    from_x = t_dot(x_ref[...], back)
    from_out = t_dot(attn_low[...], ctx)
    return jnp.concatenate(
        [from_x[:, :512], from_x[:, 512:] + from_out[:, :128], from_out[:, 128:]], axis=1
    ).astype(BF)


def attn_grad_kernel(ndp, x_ref, attn_low, back, ctx, where, slots, *rest):
    outs, held, sems = rest[:2], rest[2], rest[3]
    core = where[0, 0] % 2
    for n, (s, xx) in enumerate(((1, 0), (1, 1), (0, 0), (0, 1))):
        t = 2 * xx + (core ^ s)
        held[n] = attn_grad_of(x_ref, attn_low, back[t], ctx[t])
        store_grad(ndp, slots, s * 2 + xx, held.at[n], outs[s], sems.at[n])
    for n in range(4):
        wait(held.at[n], sems.at[n])


def whole_attn_grad_kernel(x_ref, attn_low, back, ctx, out):
    for t in range(out.shape[0]):
        out[t] = attn_grad_of(x_ref, attn_low, back[t], ctx[t])


def input_kernel(nw, back, attn_in, where, *rest):
    refs, rest = rest[:nw], rest[nw:]
    out_ref, full, total, sem = rest
    nt = back.shape[0]
    load_weights(refs, where, full, sem)
    total[...] = attn_in[...]
    for t in range(nt):
        wait(full.at[t], sem.at[t])
        total[...] += dot_t(back[t], full[t, :, 0:640])
    out_ref[...] = total[...].astype(BF)


def place_kernel(order, one, two, three, four, out, held, sem, sem_out):
    rows = one.shape[0]
    parts = (one, two, three, four)
    for n, part in enumerate(parts):
        load(part, held.at[n], sem.at[n])
    for n in range(4):
        wait(held.at[n], sem.at[n])
        spot = pl.ds(pl.multiple_of(order[n] * rows, rows), rows)
        pltpu.make_async_copy(held.at[n], out.at[spot], sem_out.at[n]).start()
    for n in range(4):
        wait(held.at[n], sem_out.at[n])


def widen_kernel(order, one, two, three, four, out, held, wide, sem, sem_out):
    rows = one.shape[0]
    half = rows // 2
    parts = (one, two, three, four)
    for n, part in enumerate(parts):
        load(part, held.at[n], sem.at[n])
    copies = [None, None]
    for n in range(len(parts)):
        wait(held.at[n], sem.at[n])
        for m in range(2):
            if copies[m] is not None:
                copies[m].wait()
            wide[m] = held[n, m * half : (m + 1) * half, :].astype(F32)
            spot = pl.ds(pl.multiple_of(order[n] * rows + m * half, half), half)
            copies[m] = pltpu.make_async_copy(wide.at[m], out.at[spot], sem_out.at[m])
            copies[m].start()
    for copy in copies:
        copy.wait()


def interleave(q, k, v, o):
    h = HEAD_DIM
    return jnp.concatenate(
        [
            q[..., : 2 * h], k[..., : 2 * h], v[..., : 2 * h],
            q[..., 2 * h :], v[..., 2 * h :], k[..., 2 * h :], o[..., 2 * h :],
            o[..., : 2 * h],
        ],
        axis=-1,
    )


def body(
    plan,
    inputs,
    segments,
    query_weight,
    key_weight,
    value_weight,
    query_bias,
    value_bias,
    out_weight,
    out_bias,
    first_gain,
    first_shift,
    inner_weight,
    inner_bias,
    outer_weight,
    outer_bias,
    second_gain,
    second_shift,
    cotangent,
):
    nt, ndp = plan.nt, plan.ndp
    width = inputs.shape[1]
    local, hidden = query_weight.shape[1], inner_weight.shape[1]
    rows = inputs.shape[0] // nt
    nseq = rows // LEN
    me = lax.axis_index("tensor")
    mine = lambda a, n: lax.dynamic_slice_in_dim(a, me * n, n, 0)
    x = mine(inputs, rows)
    cot = mine(cotangent, rows)
    seg_row = mine(segments, nseq)
    seg_col = seg_row.reshape(rows, 1)

    shards = (
        interleave(query_weight, key_weight, value_weight, out_weight.T),
        inner_weight,
        outer_weight.T,
    )
    nw = 8 if plan.pieces else 1
    if plan.pieces:
        where, slots = plan.tables()
    else:
        where = slots = jnp.zeros((1, 1), jnp.int32)
    row = lambda v: v.reshape(1, width)
    flops = 2 * rows * width * width
    limit = 28 if rows <= 512 else 56
    weights = pltpu.VMEM((nt, width, hidden), BF)
    acted = pltpu.VMEM((nt, rows, hidden), BF)
    dma = pltpu.SemaphoreType.DMA
    any_w = [anywhere()] * nw

    def attend(x, bias, attn_w):
        return call(
            functools.partial(attend_kernel, nw),
            [x, seg_row, seg_col, bias, row(out_bias), row(first_gain), row(first_shift), where, *attn_w],
            [vmem()] * 7 + [smem()] + any_w,
            [
                shape((nt, rows, 640), BF),
                shape((nt, nseq, 3, LEN, LEN), BF),
                shape((nt, rows, 256), BF),
                shape((rows, width), F32),
                shape((rows, 128), F32),
                shape((rows, width), BF),
            ],
            [vmem()] * 6,
            [weights, pltpu.VMEM((nseq, LEN, LEN), F32), dma((nt,))],
            limit,
            8 * flops,
        )

    def inner(low, inner_b, inner_w):
        return call(
            functools.partial(inner_kernel, nw),
            [low, inner_b, where, *inner_w],
            [vmem()] * 2 + [smem()] + any_w,
            [shape((nt, rows, hidden), BF)] * 2,
            [vmem()] * 2,
            [weights, pltpu.VMEM((rows, hidden), F32), dma((nt,))],
            limit,
            8 * flops,
        )

    def outer(active, normed, outer_w):
        return call(
            functools.partial(outer_kernel, nw),
            [
                active, normed, row(first_gain), row(first_shift), row(outer_bias),
                row(second_gain), row(second_shift), cot, where, *outer_w,
            ],
            [anywhere()] + [vmem()] * 7 + [smem()] + any_w,
            [shape((rows, width), BF), shape((rows, width), F32), shape((rows, width), BF), shape((8, width), F32)],
            [vmem()] * 4,
            [weights, acted, dma((nt,)), dma((nt,))],
            limit,
            4 * flops,
        )

    def dinner(ffn_low, slope, outer_w):
        return call(
            functools.partial(slope_kernel, nw),
            [ffn_low, slope, where, *outer_w],
            [vmem(), anywhere(), smem()] + any_w,
            [shape((nt, rows, hidden), BF), shape((nt, 1, hidden), F32)],
            [vmem()] * 2,
            [weights, acted, dma((nt,)), dma((nt,))],
            limit,
            4 * flops,
        )

    def grad(side, left, right):
        return call(
            functools.partial(grad_kernel, ndp, side),
            [left, right, where, slots],
            [vmem(), anywhere(), smem(), smem()],
            [shape((4, plan.nz, width // ndp, hidden), BF)],
            [anywhere()],
            [pltpu.VMEM((2, rows, hidden), BF), pltpu.VMEM((2, width, hidden), BF), dma((2,)), dma((2,))],
            limit,
            2 * flops,
        )[0]

    def whole_grad(left, right):
        return call(
            whole_grad_kernel, [left, right], [vmem()] * 2, [shape((nt, width, hidden), BF)], [vmem()], [], limit, 4 * flops
        )[0]

    def first(pulled, second, normed, scale, inner_w, attn_w):
        return call(
            functools.partial(first_kernel, nw),
            [pulled, second, normed, scale, row(first_gain), where, *inner_w, *attn_w],
            [anywhere()] + [vmem()] * 4 + [smem()] + any_w * 2,
            [shape((rows, width), F32), shape((rows, width), BF), shape((nt, rows, 256), BF), shape((8, width), F32)],
            [vmem()] * 4,
            [weights, weights, acted, dma((nt,)), dma((nt,)), dma((nt,))],
            limit,
            6 * flops,
        )

    def attend_pull(acts, probs, ctx_grad):
        return call(
            attend_pull_kernel,
            [acts, probs, ctx_grad],
            [vmem()] * 3,
            [shape((nt, rows, 640), BF), shape((nt, 1, 640), F32)],
            [vmem()] * 2,
            [],
            limit,
            8 * flops,
        )

    def attn_grad(attn_low, back, ctx):
        return call(
            functools.partial(attn_grad_kernel, ndp),
            [x, attn_low, back, ctx, where, slots],
            [vmem()] * 4 + [smem()] * 2,
            [shape((4, plan.nz, width // ndp, hidden), BF)] * 2,
            [anywhere()] * 2,
            [pltpu.VMEM((4, width, hidden), BF), dma((4,))],
            limit,
            4 * flops,
        )

    def whole_attn_grad(attn_low, back, ctx):
        return call(
            whole_attn_grad_kernel,
            [x, attn_low, back, ctx],
            [vmem()] * 4,
            [shape((nt, width, hidden), BF)],
            [vmem()],
            [],
            limit,
            4 * flops,
        )[0]

    def input_part(back, attn_in, attn_w):
        return call(
            functools.partial(input_kernel, nw),
            [back, attn_in, where, *attn_w],
            [vmem()] * 2 + [smem()] + any_w,
            [shape((rows, width), BF)],
            [vmem()],
            [weights, pltpu.VMEM((rows, width), F32), dma((nt,))],
            limit,
            4 * flops,
        )[0]

    def place(parts):
        order = jnp.stack([me, me ^ 2, me ^ 1, me ^ 3]).astype(jnp.int32)
        return call(
            place_kernel,
            [order, *parts],
            [smem()] + [anywhere()] * 4,
            [shape((nt * rows, width), BF)],
            [anywhere()],
            [pltpu.VMEM((4, rows, width), BF), dma((4,)), dma((4,))],
            limit,
            flops // 8,
        )[0]

    def widen(parts):
        order = jnp.stack([me, me ^ 2, me ^ 1, me ^ 3]).astype(jnp.int32)
        return call(
            widen_kernel,
            [order, *parts],
            [smem()] + [anywhere()] * 4,
            [shape((nt * rows, width), F32)],
            [anywhere()],
            [pltpu.VMEM((4, rows, width), BF), pltpu.VMEM((2, rows // 2, width), F32), dma((4,)), dma((2,))],
            limit,
            flops // 4,
        )[0]

    def small_parts():
        every = lax.all_gather(jnp.concatenate([query_bias, value_bias, inner_bias]), "tensor", axis=0)
        q_b, v_b = every[:, None, :local], every[:, None, local : 2 * local]
        none = jnp.zeros_like(q_b)
        return interleave(q_b, none, v_b, none), every[:, None, 2 * local :]

    bias, inner_b = small_parts()
    if plan.pieces:
        turn, one_way, other_way, core = plan.turn, plan.first(), plan.second(), plan.core()

        def spread(own):
            return [own, turn(own, one_way), turn(own, other_way)]

        def rest_of(three):
            mine = three + [turn(three[1], other_way)]
            return mine, lambda: mine + [turn(v, core) for v in mine]

        own1 = plan.near(shards[0])
        own1, bias, inner_b = lax.optimization_barrier((own1, bias, inner_b))
        own23 = plan.near(jnp.concatenate([shards[1], shards[2]], axis=1))
        own2, own3 = own23[..., :hidden], own23[..., hidden:]
        three1 = spread(own1)
        mine1, all1 = rest_of(three1)
        three2 = spread(tie(own2, mine1[3]))
        attn_w = all1()
        acts, probs, ctx, normed, scale, low = attend(x, bias, attn_w)
        three2 = list(lax.optimization_barrier((*three2, low))[:3])
        mine2, all2 = rest_of(three2)
        three3 = spread(tie(own3, mine2[3]))
        inner_w = all2()
        active, slope = inner(low, inner_b, inner_w)
        three3 = list(lax.optimization_barrier((*three3, active))[:3])
        mine3, all3 = rest_of(three3)
        outer_w = all3()
        layer_part, second, ffn_low, second_vec = outer(active, normed, outer_w)

        send3 = grad(1, ffn_low, active)
        got3 = turn(send3, core)
        layer_parts = plan.share(layer_part)
        keep3 = grad(0, ffn_low, tie(active, send3))
        pulled, inner_vec = dinner(tie(ffn_low, keep3), slope, outer_w)
        got3 = tie(got3, pulled)
        away3, go3a = plan.scatter_a(keep3, got3)
        got3a = go3a()
        low_t = tie(low, away3)
        send2 = grad(1, low_t, pulled)
        got2 = turn(send2, core)
        keep2 = grad(0, low_t, tie(pulled, send2))
        attn_in, attn_low, ctx_grad, first_vec = first(
            pulled, tie(second, keep2), normed, scale, inner_w, attn_w
        )
        got3a = tie(got3a, attn_low)
        away3b, go3b = plan.scatter_b(keep3, got3, got3a)
        got3b = go3b()
        got2 = tie(got2, away3b)
        away2, go2a = plan.scatter_a(keep2, got2)
        got2a = go2a()
        back, back_vec = attend_pull(acts, probs, tie(ctx_grad, away2))
        got3b = tie(got3b, back)
        outer_grad = plan.scatter_z(keep3, got3, got3a, got3b)
        keep1, send1 = attn_grad(attn_low, back, ctx)
        got1 = turn(send1, core)
        layer_out = place(layer_parts)
        got2a = tie(got2a, keep1)
        away2b, go2b = plan.scatter_b(keep2, got2, got2a)
        got2b = go2b()
        input_low = input_part(tie(back, away2b), attn_in, attn_w)
        got1 = tie(got1, input_low)
        away1, go1a = plan.scatter_a(keep1, got1)
        got1a = go1a()
        inner_grad = plan.scatter_z(keep2, got2, got2a, tie(got2b, away1))
        away1b, go1b = plan.scatter_b(keep1, got1, got1a)
        got1b = go1b()
        input_parts = plan.share(tie(input_low, away1b))
        attn_g = plan.scatter_z(keep1, got1, got1a, got1b)
        input_grad = widen(input_parts)
    else:
        attn_w, inner_w, outer_w = (
            [lax.all_gather(lax.all_gather(s, "dp", axis=0, tiled=True), "tensor", axis=0)]
            for s in shards
        )
        acts, probs, ctx, normed, scale, low = attend(x, bias, attn_w)
        active, slope = inner(low, inner_b, inner_w)
        layer_part, second, ffn_low, second_vec = outer(active, normed, outer_w)
        pulled, inner_vec = dinner(ffn_low, slope, outer_w)
        attn_in, attn_low, ctx_grad, first_vec = first(pulled, second, normed, scale, inner_w, attn_w)
        back, back_vec = attend_pull(acts, probs, ctx_grad)
        input_low = input_part(back, attn_in, attn_w)
        outer_grad, inner_grad, attn_g = (
            lax.psum_scatter(
                lax.psum_scatter(g, "tensor", scatter_dimension=0, tiled=False),
                "dp",
                scatter_dimension=0,
                tiled=True,
            ).astype(F32)
            for g in (whole_grad(ffn_low, active), whole_grad(low, pulled), whole_attn_grad(attn_low, back, ctx))
        )
        layer_out = lax.all_gather(layer_part, "tensor", axis=0, tiled=True)
        input_grad = lax.all_gather(input_low, "tensor", axis=0, tiled=True).astype(F32)

    h = HEAD_DIM
    vectors = jnp.concatenate(
        [
            second_vec[:3].reshape(-1),
            first_vec[:3].reshape(-1),
            inner_vec.reshape(-1),
            back_vec.reshape(-1),
        ]
    ).reshape(-1, 128)
    vectors = plan.total(vectors) if plan.pieces else lax.psum(vectors, AXES)
    flat = vectors.reshape(-1)
    gain2, shift2, bias2, gain1, shift1, bias1 = (flat[i * width : (i + 1) * width] for i in range(6))
    at = 6 * width
    inner_bias_grad = lax.dynamic_slice_in_dim(flat, at + me * hidden, hidden, 0)
    at += nt * hidden
    mine_vec = lax.dynamic_slice_in_dim(flat, at + me * 640, 640, 0)
    query_bias_grad = jnp.concatenate([mine_vec[: 2 * h], mine_vec[6 * h : 7 * h]])
    value_bias_grad = jnp.concatenate([mine_vec[4 * h : 6 * h], mine_vec[7 * h : 8 * h]])
    part = lambda *spans: jnp.concatenate([attn_g[:, a * h : b * h] for a, b in spans], axis=1)
    return (
        layer_out,
        input_grad,
        part((0, 2), (6, 7)),
        part((2, 4), (8, 9)),
        part((4, 6), (7, 8)),
        query_bias_grad,
        value_bias_grad,
        part((10, 12), (9, 10)).T,
        bias1,
        gain1,
        shift1,
        inner_grad,
        inner_bias_grad,
        outer_grad.T,
        bias2,
        gain2,
        shift2,
    )


def solution(mesh):
    in_specs = (
        P("dp", None),
        P("dp", None),
        P("dp", "tensor"),
        P("dp", "tensor"),
        P("dp", "tensor"),
        P("tensor"),
        P("tensor"),
        P("tensor", "dp"),
        P(),
        P(),
        P(),
        P("dp", "tensor"),
        P("tensor"),
        P("tensor", "dp"),
        P(),
        P(),
        P(),
        P("dp", None),
    )
    out_specs = (
        P("dp", None),
        P("dp", None),
        P("dp", "tensor"),
        P("dp", "tensor"),
        P("dp", "tensor"),
        P("tensor"),
        P("tensor"),
        P("tensor", "dp"),
        P(),
        P(),
        P(),
        P("dp", "tensor"),
        P("tensor"),
        P("tensor", "dp"),
        P(),
        P(),
        P(),
    )
    return jax.shard_map(
        functools.partial(body, Plan(mesh)),
        mesh=mesh,
        in_specs=in_specs,
        out_specs=out_specs,
        check_vma=False,
    )
```

time: 956 us -> 325 us (0.34)
  waiting for transfers between devices: 508 us -> 92.7 us
  blocking collectives: 165 us -> 5.18 us
  matrix products: 134 us -> 0 us
  Pallas kernels: 0 us -> 112 us
  starting transfers between devices: 1.55 us -> 56.3 us
  local copies, waits for them, and re-layouts: 73 us -> 31.3 us
  other arithmetic: 48.2 us -> 21.5 us
  between operations: 16.2 us -> 1.92 us
    psum x4 -> x0, waiting for transfers between devices: 205 us -> none  [the longest x1 68.5 us: body(): lax.psum(matmul_right(grad_inner, inner_full).astype(jnp.bfloat16), 'tens...]
    unnamed x16 -> x0, waiting for transfers between devices: 159 us -> none
    reduce_scatter x2 -> x0, waiting for transfers between devices: 144 us -> none  [the longest x1 72.2 us: body(): lax.psum_scatter(outer_local, 'dp', scatter_dimension=1, tiled=True)]
    dot_general x45 -> x0, matrix products: 131 us -> none  [the longest x6 38.6 us: matmul(): return jnp.dot(left, right, preferred_element_type=jnp.float32)]
    all_gather x4 -> x1, blocking collectives: 127 us -> 5.18 us  [small_parts(): lax.all_gather(jnp.concatenate([query_bias, value_bias, inner_bias]), 'te...]
    pallas_call x0 -> x14, Pallas kernels: none -> 112 us  [call(): pl.pallas_call(body, out_shape=outs, in_specs=in_specs, out_specs=out_spe...]
    ppermute x0 -> x57, waiting for transfers between devices: none -> 92.7 us  [turn(): return lax.ppermute(values, AXES, pairs)]
    ppermute x0 -> x57, starting transfers between devices: none -> 56.3 us  [turn(): return lax.ppermute(values, AXES, pairs)]
  transfers between devices with their start and end apart: 12 -> 57, of which waited for: 8 -> 17; matrix products, arithmetic and copies ran while one was open for 9% -> 8% of each run, Pallas kernels for 0% -> 27%
where the time goes in v1:
time: 325 us; the launch traced here: 321 us
  Pallas kernels  112 us (34%)
  waiting for transfers between devices  92.7 us (29%)
  starting transfers between devices  56.3 us (17%)
  local copies, waits for them, and re-layouts  31.3 us (10%)
  other arithmetic  21.5 us (7%)
  blocking collectives  5.18 us (2%)
    pallas_call x14, Pallas kernels, call(): pl.pallas_call(body, out_shape=outs, in_specs=in_specs, out_specs=out_spe...  112 us
    ppermute x57, waiting for transfers between devices, turn(): return lax.ppermute(values, AXES, pairs)  92.7 us
    ppermute x57, starting transfers between devices, turn(): return lax.ppermute(values, AXES, pairs)  56.3 us
    unnamed x123, local copies, waits for them, and re-layouts  21.1 us
  transfers between devices with their start and end apart: 57, of which 17 were waited for; matrix products, arithmetic and copies ran while one was open for 8% of the time, Pallas kernels for 27%

profile of v1, /device:TPU:0, one launch (start us, length us, event | category | flops | bytes accessed | tf_op | source)
XLA Modules:
  0.0 321.2 jit_solution(14335556901173161495)
XLA Ops:
  6.3 3.1 collective-permute-start
  9.4 2.6 collective-permute-start.1
  12.8 5.2 %all-gather.1 = f32[4,1,1152]{2,1,0:T(1,128)S(1)} all-gather(f32[1,1,1152]{2,1,0:T(1,128)S(1)} %reshape.308), channel_id=2, replica_groups=mesh['dp'=8,'tensor'=4] {'tensor'}, dimensions={0}, use_global_device_ids=true | all-gather | bytes 23040 | tf_op jit(solution)/shard_map/all_gather | solution.py:723
  18.2 5.3 %collective-permute-done.1 = bf16[96,768]{1,0:T(8,128)(2,1)} collective-permute-done((bf16[96,768]{1,0:T(8,128)(2,1)S(1)}, bf16[96,768]{1,0:T(8,128)(2,1)}, u32[]{:S(2)}, u32[]{:S(2)}) %collective-permute-start.1) | collective-permute-done | bytes 147488 | tf_op jit(solution)/shard_map/ppermute | solution.py:109
  23.5 2.0 pad_maximum_fusion.4.rest_0_.rest_8_
  25.5 1.5 collective-permute-start.3
  27.8 2.3 collective-permute-start.10
  31.1 1.5 collective-permute-start.12
  32.7 1.5 collective-permute-start.4
  34.2 6.8 %collective-permute-done.10 = bf16[96,1536]{1,0:T(8,128)(2,1)} collective-permute-done((bf16[96,1536]{1,0:T(8,128)(2,1)}, bf16[96,1536]{1,0:T(8,128)(2,1)}, u32[]{:S(2)}, u32[]{:S(2)}) %collective-permute-start.10) | collective-permute-done | bytes 294944 | tf_op jit(solution)/shard_map/ppermute | solution.py:109
  41.0 12.9 %collective-permute-done.11 = bf16[96,1536]{1,0:T(8,128)(2,1)} collective-permute-done((bf16[96,1536]{1,0:T(8,128)(2,1)}, bf16[96,1536]{1,0:T(8,128)(2,1)}, u32[]{:S(2)}, u32[]{:S(2)}) %collective-permute-start.11) | collective-permute-done | bytes 294944 | tf_op jit(solution)/shard_map/ppermute | solution.py:109
  53.9 1.4 pad_maximum_fusion
  57.5 1.5 collective-permute-start.14
  60.6 1.6 collective-permute-done.9.rest_7_.rest_15_
  62.2 11.5 %shard_map.305 = (bf16[4,512,640]{2,1,0:T(8,128)(2,1)S(1)}, bf16[4,2,3,256,256]{4,3,2,1,0:T(8,128)(2,1)S(1)}, bf16[4,512,256]{2,1,0:T(8,128)(2,1)S(1)}, f32[512,...) custom-call(bf16[512,768]{1,0:T(8,128)(2,1)S(1)} %constant_dynamic-slice_fusion.2.x_ref, ...), custom_call_target="tpu_custom_call" | custom-call | flops 1000 | bytes 1000 | tf_op jit(solution)/shard_map/pallas_call | solution.py:45
  73.8 1.7 copy-done.16
  75.4 1.5 copy-done.18
  79.2 1.4 collective-permute-start.16
  81.0 7.7 %collective-permute-done.15.rest_3_ = bf16[4,96,768]{2,1,0:T(8,128)(2,1)S(1)} collective-permute-done((bf16[4,96,768]{2,1,0:T(8,128)(2,1)}, bf16[4,96,768]{2,1,0:T(8,128)(2,1)S(1)}, u32[]{:S(2)}, u32[]{:S(2)}) %collective-permute-start.15) | collective-permute-done | bytes 589856 | tf_op jit(solution)/shard_map/ppermute | solution.py:109
  91.1 16.4 %shard_map.306 = (bf16[4,512,768]{2,1,0:T(8,128)(2,1)S(1)}, bf16[4,512,768]{2,1,0:T(8,128)(2,1)S(1)}) custom-call(bf16[512,768]{1,0:T(8,128)(2,1)S(1)} %get-tuple-element.89.low_ref.left, f32[4,1,768]{2,1,0:T(1,128)S(1)} %broadcast_in_dim.109.bias, s32[2,32]{1,0:T(2,128)S(1)} %pad_add_fusion.where, bf16[4,96,768]{2,1,0:T(8,128)(2,1)} %get-tuple-element.70.rest_0_, ...), custom_call_target="tpu_custom_call" | custom-call | flops 1000 | bytes 1000 | tf_op jit(solution)/shard_map/pallas_call | solution.py:45
  107.6 1.7 copy-done.14
  110.6 8.9 %collective-permute-done.22.rest_3_ = bf16[4,96,768]{2,1,0:T(8,128)(2,1)} collective-permute-done((bf16[4,96,768]{2,1,0:T(8,128)(2,1)}, bf16[4,96,768]{2,1,0:T(8,128)(2,1)}, u32[]{:S(2)}, u32[]{:S(2)}) %collective-permute-start.22) | collective-permute-done | bytes 589856 | tf_op jit(solution)/shard_map/ppermute | solution.py:109
  119.8 1.3 constant_dynamic-slice_fusion.cot
  121.8 8.8 %shard_map.307 = (bf16[512,768]{1,0:T(8,128)(2,1)}, f32[512,768]{1,0:T(8,128)S(1)}, bf16[512,768]{1,0:T(8,128)(2,1)S(1)}, f32[8,768]{1,0:T(8,128)S(1)}) custom-call(bf16[4,512,768]{2,1,0:T(8,128)(2,1)S(1)} %get-tuple-element.83.active.right, f32[512,768]{1,0:T(8,128)S(1)} %copy-done.10, f32[1,768]{1,0:T(1,128)S(1)} %reshape.296.gain.gain1, ...), custom_call_target="tpu_custom_call" | custom-call | flops 1000 | bytes 1000 | tf_op jit(solution)/shard_map/pallas_call | solution.py:45
  130.6 5.9 %shard_map.309 = bf16[4,4,96,768]{3,2,1,0:T(8,128)(2,1)S(1)} custom-call(bf16[512,768]{1,0:T(8,128)(2,1)S(1)} %get-tuple-element.84.left.ffn_ref, bf16[4,512,768]{2,1,0:T(8,128)(2,1)S(1)} %get-tuple-element.83.active.right, s32[2,32]{1,0:T(2,128)S(1)} %pad_add_fusion.where, s32[4,8]{1,0:T(4,128)S(1)} %multiply_add_fusion.slots), custom_call_target="tpu_custom_call" | custom-call | flops 1000 | bytes 1000 | tf_op jit(solution)/shard_map/pallas_call | solution.py:45
  137.5 5.9 %shard_map.310 = bf16[4,4,96,768]{3,2,1,0:T(8,128)(2,1)S(1)} custom-call(bf16[512,768]{1,0:T(8,128)(2,1)S(1)} %get-tuple-element.84.left.ffn_ref, bf16[4,512,768]{2,1,0:T(8,128)(2,1)S(1)} %get-tuple-element.83.active.right, s32[2,32]{1,0:T(2,128)S(1)} %pad_add_fusion.where, s32[4,8]{1,0:T(4,128)S(1)} %multiply_add_fusion.slots), custom_call_target="tpu_custom_call" | custom-call | flops 1000 | bytes 1000 | tf_op jit(solution)/shard_map/pallas_call | solution.py:45
  143.5 6.4 %shard_map.311 = (bf16[4,512,768]{2,1,0:T(8,128)(2,1)S(1)}, f32[4,1,768]{2,1,0:T(1,128)S(1)}) custom-call(bf16[512,768]{1,0:T(8,128)(2,1)S(1)} %get-tuple-element.84.left.ffn_ref, bf16[4,512,768]{2,1,0:T(8,128)(2,1)S(1)} %copy-done.15, s32[2,32]{1,0:T(2,128)S(1)} %pad_add_fusion.where, bf16[4,96,768]{2,1,0:T(8,128)(2,1)} %get-tuple-element.76.rest_0_, ...), custom_call_target="tpu_custom_call" | custom-call | flops 1000 | bytes 1000 | tf_op jit(solution)/shard_map/pallas_call | solution.py:45
  150.3 1.6 copy-done.6
  151.9 5.9 %shard_map.312 = bf16[4,4,96,768]{3,2,1,0:T(8,128)(2,1)S(1)} custom-call(bf16[512,768]{1,0:T(8,128)(2,1)S(1)} %copy-done.6, bf16[4,512,768]{2,1,0:T(8,128)(2,1)S(1)} %get-tuple-element.90.right.pulled, s32[2,32]{1,0:T(2,128)S(1)} %pad_add_fusion.where, s32[4,8]{1,0:T(4,128)S(1)} %multiply_add_fusion.slots), custom_call_target="tpu_custom_call" | custom-call | flops 1000 | bytes 1000 | tf_op jit(solution)/shard_map/pallas_call | solution.py:45
  160.8 5.9 %shard_map.313 = bf16[4,4,96,768]{3,2,1,0:T(8,128)(2,1)S(1)} custom-call(bf16[512,768]{1,0:T(8,128)(2,1)S(1)} %copy-done.6, bf16[4,512,768]{2,1,0:T(8,128)(2,1)S(1)} %get-tuple-element.90.right.pulled, s32[2,32]{1,0:T(2,128)S(1)} %pad_add_fusion.where, s32[4,8]{1,0:T(4,128)S(1)} %multiply_add_fusion.slots), custom_call_target="tpu_custom_call" | custom-call | flops 1000 | bytes 1000 | tf_op jit(solution)/shard_map/pallas_call | solution.py:45
  166.8 13.0 %shard_map.314 = (f32[512,768]{1,0:T(8,128)S(1)}, bf16[512,768]{1,0:T(8,128)(2,1)S(1)}, bf16[4,512,256]{2,1,0:T(8,128)(2,1)S(1)}, f32[8,768]{1,0:T(8,128)S(1)}) custom-call(bf16[4,512,768]{2,1,0:T(8,128)(2,1)S(1)} %get-tuple-element.90.right.pulled, f32[512,768]{1,0:T(8,128)S(1)} %get-tuple-element.91.second, f32[512,768]{1,0:T(8,128)S(1)} %copy-done.10, ...), custom_call_target="tpu_custom_call" | custom-call | flops 1000 | bytes 1000 | tf_op jit(solution)/shard_map/pallas_call | solution.py:45
  179.8 3.4 %collective-permute-done.32 = bf16[2,4,96,768]{3,2,1,0:T(8,128)(2,1)S(1)} collective-permute-done((bf16[2,4,96,768]{3,2,1,0:T(8,128)(2,1)S(1)}, bf16[2,4,96,768]{3,2,1,0:T(8,128)(2,1)S(1)}, u32[]{:S(2)}, u32[]{:S(2)}) %collective-permute-start.32) | collective-permute-done | bytes 1179680 | tf_op jit(solution)/shard_map/ppermute | solution.py:109
  188.4 8.5 %shard_map.315 = (bf16[4,512,640]{2,1,0:T(8,128)(2,1)S(1)}, f32[4,1,640]{2,1,0:T(1,128)S(1)}) custom-call(bf16[4,512,640]{2,1,0:T(8,128)(2,1)S(1)} %copy-done.19, bf16[4,2,3,256,256]{4,3,2,1,0:T(8,128)(2,1)S(1)} %copy-done.17, bf16[4,512,256]{2,1,0:T(8,128)(2,1)S(1)} %get-tuple-element.97.ctx_grad), custom_call_target="tpu_custom_call" | custom-call | flops 1000 | bytes 1000 | tf_op jit(solution)/shard_map/pallas_call | solution.py:45
  196.9 7.5 %shard_map.316 = (bf16[4,4,96,768]{3,2,1,0:T(8,128)(2,1)S(1)}, bf16[4,4,96,768]{3,2,1,0:T(8,128)(2,1)}) custom-call(bf16[512,768]{1,0:T(8,128)(2,1)S(1)} %copy-done.8, bf16[512,768]{1,0:T(8,128)(2,1)S(1)} %get-tuple-element.94.attn_low, bf16[4,512,640]{2,1,0:T(8,128)(2,1)S(1)} %get-tuple-element.102.back, bf16[4,512,256]{2,1,0:T(8,128)(2,1)S(1)} %copy-done.35, ...), custom_call_target="tpu_custom_call" | custom-call | flops 1000 | bytes 1000 | tf_op jit(solution)/shard_map/pallas_call | solution.py:45
  204.4 1.5 copy-done.30
  207.3 1.4 collective-permute-start.33
  208.7 3.2 collective-permute-done.28.three
  213.0 3.4 %shard_map.308 = bf16[2048,768]{1,0:T(8,128)(2,1)} custom-call(s32[4]{0:T(128)S(1)} %pad_add_fusion.1.order, bf16[512,768]{1,0:T(8,128)(2,1)} %get-tuple-element.79.one, bf16[512,768]{1,0:T(8,128)(2,1)} %collective-permute-done.27.two, bf16[512,768]{1,0:T(8,128)(2,1)} %collective-permute-done.28.three, bf16[512,768]{1,0:T(8,128)(2,1)} %collective-permute-done.29.four), custom_call_target="tpu_custom_call" | custom-call | flops 1000 | bytes 1000 | tf_op jit(solution)/shard_map/pallas_call | solution.py:45
  216.4 6.2 %collective-permute-done.53 = bf16[4,96,768]{2,1,0:T(8,128)(2,1)} collective-permute-done((bf16[4,96,768]{2,1,0:T(8,128)(2,1)}, bf16[4,96,768]{2,1,0:T(8,128)(2,1)}, u32[]{:S(2)}, u32[]{:S(2)}) %collective-permute-start.53) | collective-permute-done | bytes 589856 | tf_op jit(solution)/shard_map/ppermute | solution.py:109
  223.7 1.9 fusion.14
  225.6 3.5 %collective-permute-done.44 = f32[80,128]{1,0:T(8,128)S(1)} collective-permute-done((f32[80,128]{1,0:T(8,128)S(1)}, f32[80,128]{1,0:T(8,128)S(1)}, u32[]{:S(2)}, u32[]{:S(2)}) %collective-permute-start.44) | collective-permute-done | bytes 40992 | tf_op jit(solution)/shard_map/ppermute | solution.py:109
  230.1 4.5 %collective-permute-start.54 = (bf16[96,768]{1,0:T(8,128)(2,1)S(1)}, bf16[96,768]{1,0:T(8,128)(2,1)S(1)}, u32[]{:S(2)}, u32[]{:S(2)}) collective-permute-start(bf16[96,768]{1,0:T(8,128)(2,1)S(1)} %get-tuple-element.178), channel_id=1, source_target_pairs={{0,8},{1,9},{2,10},{3,11},{4,12},{5,13},{6,14},{7,15},{8,0},{9,1},... | collective-permute-start | bytes 442376 | tf_op jit(solution)/shard_map/ppermute | solution.py:109
  234.6 1.3 collective-permute-start.55
  235.8 1.4 collective-permute-start.56
  237.2 1.9 collective-permute-start.46
  239.1 1.4 fusion.1
  240.7 7.0 %shard_map.317.one = bf16[512,768]{1,0:T(8,128)(2,1)} custom-call(bf16[4,512,640]{2,1,0:T(8,128)(2,1)S(1)} %get-tuple-element.102.back, f32[512,768]{1,0:T(8,128)S(1)} %copy-done.33, s32[2,32]{1,0:T(2,128)S(1)} %pad_add_fusion.where, bf16[4,96,768]{2,1,0:T(8,128)(2,1)} %pad_maximum_fusion.4.rest_0_.rest_8_, ...), custom_call_target="tpu_custom_call" | custom-call | flops 1000 | bytes 1000 | tf_op jit(solution)/shard_map/pallas_call | solution.py:45
  247.8 1.3 collective-permute-start.47
  249.0 1.6 add_convert_fusion.2
  250.7 1.5 collective-permute-start.48
  252.2 1.4 collective-permute-start.35
  254.4 2.2 collective-permute-done.48
  258.8 15.9 %collective-permute-done.35 = bf16[2,4,96,768]{3,2,1,0:T(8,128)(2,1)S(1)} collective-permute-done((bf16[2,4,96,768]{3,2,1,0:T(8,128)(2,1)S(1)}, bf16[2,4,96,768]{3,2,1,0:T(8,128)(2,1)S(1)}, u32[]{:S(2)}, u32[]{:S(2)}) %collective-permute-start.35) | collective-permute-done | bytes 1179680 | tf_op jit(solution)/shard_map/ppermute | solution.py:109
  274.7 1.3 fusion.2
  278.3 1.4 fusion.15
  280.9 1.7 collective-permute-start.51
  282.6 1.5 collective-permute-start.52
  284.2 1.4 collective-permute-start.36
  285.9 1.4 fusion.16
  288.3 2.1 collective-permute-start.41
  290.4 4.2 %collective-permute-done.51 = bf16[96,768]{1,0:T(8,128)(2,1)S(1)} collective-permute-done((bf16[96,768]{1,0:T(8,128)(2,1)S(1)}, bf16[96,768]{1,0:T(8,128)(2,1)S(1)}, u32[]{:S(2)}, u32[]{:S(2)}) %collective-permute-start.51) | collective-permute-done | bytes 147488 | tf_op jit(solution)/shard_map/ppermute | solution.py:109
  294.7 1.6 collective-permute-start.42
  297.1 8.8 %collective-permute-done.41 = bf16[96,768]{1,0:T(8,128)(2,1)S(1)} collective-permute-done((bf16[96,768]{1,0:T(8,128)(2,1)S(1)}, bf16[96,768]{1,0:T(8,128)(2,1)S(1)}, u32[]{:S(2)}, u32[]{:S(2)}) %collective-permute-start.41) | collective-permute-done | bytes 147488 | tf_op jit(solution)/shard_map/ppermute | solution.py:109
  314.9 6.0 %shard_map.318 = f32[2048,768]{1,0:T(8,128)} custom-call(s32[4]{0:T(128)S(1)} %pad_add_fusion.1.order, bf16[512,768]{1,0:T(8,128)(2,1)} %shard_map.317.one, bf16[512,768]{1,0:T(8,128)(2,1)S(1)} %copy-done.37, bf16[512,768]{1,0:T(8,128)(2,1)S(1)} %copy-done.39, bf16[512,768]{1,0:T(8,128)(2,1)S(1)} %copy-done.41), custom_call_target="tpu_custom_call" | custom-call | flops 1000 | bytes 1000 | tf_op jit(solution)/shard_map/pallas_call | solution.py:45
  (281 shorter events, 51.5 us)
Async XLA Ops:
  0.7 59.8 %copy-start = (bf16[2048,768]{1,0:T(8,128)(2,1)S(1)}, bf16[2048,768]{1,0:T(8,128)(2,1)}, u32[]{:S(2)}) copy-start(bf16[2048,768]{1,0:T(8,128)(2,1)} %param.18) | copy-start | bytes 9437188
  6.3 11.9 %collective-permute-start = (bf16[96,768]{1,0:T(8,128)(2,1)S(1)}, bf16[96,768]{1,0:T(8,128)(2,1)}, u32[]{:S(2)}, u32[]{:S(2)}) collective-permute-start(bf16[96,768]{1,0:T(8,128)(2,1)S(1)} %concatenate.36), channel_id=1, source_target_pairs={{0,8},{1,9},{2,10},{3,11},{4,12},{5,13},{6,14},{7,15},{8,0},{9,1},... | collective-permute-start | bytes 442376 | tf_op jit(solution)/shard_map/ppermute | solution.py:109
  9.4 14.1 %collective-permute-start.1 = (bf16[96,768]{1,0:T(8,128)(2,1)S(1)}, bf16[96,768]{1,0:T(8,128)(2,1)}, u32[]{:S(2)}, u32[]{:S(2)}) collective-permute-start(bf16[96,768]{1,0:T(8,128)(2,1)S(1)} %concatenate.36), channel_id=1, source_target_pairs={{0,16},{1,17},{2,18},{3,19},{4,20},{5,21},{6,22},{7,23},{8,24},{9,... | collective-permute-start | bytes 442376 | tf_op jit(solution)/shard_map/ppermute | solution.py:109
  12.0 11.5 %collective-permute-start.2 = (bf16[96,768]{1,0:T(8,128)(2,1)S(1)}, bf16[96,768]{1,0:T(8,128)(2,1)}, u32[]{:S(2)}, u32[]{:S(2)}) collective-permute-start(bf16[96,768]{1,0:T(8,128)(2,1)S(1)} %concatenate.36), channel_id=1, source_target_pairs={{0,24},{1,25},{2,26},{3,27},{4,28},{5,29},{6,30},{7,31},{8,16},{9,... | collective-permute-start | bytes 442376 | tf_op jit(solution)/shard_map/ppermute | solution.py:109
  25.5 15.5 %collective-permute-start.3 = (bf16[4,96,768]{2,1,0:T(8,128)(2,1)}, bf16[4,96,768]{2,1,0:T(8,128)(2,1)}, u32[]{:S(2)}, u32[]{:S(2)}) collective-permute-start(bf16[4,96,768]{2,1,0:T(8,128)(2,1)} %pad_maximum_fusion.4.rest_0_.rest_8_), channel_id=1, source_target_pairs={{0,2},{1,5},{2,0},{3,7},{4,6},{5,1},{6,4},{7,3},{8,10},{9,13},{10,... | collective-permute-start | bytes 1769480 | tf_op jit(solution)/shard_map/ppermute | solution.py:109
  27.8 13.2 %collective-permute-start.10 = (bf16[96,1536]{1,0:T(8,128)(2,1)}, bf16[96,1536]{1,0:T(8,128)(2,1)}, u32[]{:S(2)}, u32[]{:S(2)}) collective-permute-start(bf16[96,1536]{1,0:T(8,128)(2,1)} %get-tuple-element.196), channel_id=1, source_target_pairs={{0,8},{1,9},{2,10},{3,11},{4,12},{5,13},{6,14},{7,15},{8,0},{9,1},... | collective-permute-start | bytes 884744 | tf_op jit(solution)/shard_map/ppermute | solution.py:109
  30.1 23.8 %collective-permute-start.11 = (bf16[96,1536]{1,0:T(8,128)(2,1)}, bf16[96,1536]{1,0:T(8,128)(2,1)}, u32[]{:S(2)}, u32[]{:S(2)}) collective-permute-start(bf16[96,1536]{1,0:T(8,128)(2,1)} %get-tuple-element.196), channel_id=1, source_target_pairs={{0,16},{1,17},{2,18},{3,19},{4,20},{5,21},{6,22},{7,23},{8,24},{9,... | collective-permute-start | bytes 884744 | tf_op jit(solution)/shard_map/ppermute | solution.py:109
  31.1 22.8 %collective-permute-start.12 = (bf16[96,1536]{1,0:T(8,128)(2,1)}, bf16[96,1536]{1,0:T(8,128)(2,1)}, u32[]{:S(2)}, u32[]{:S(2)}) collective-permute-start(bf16[96,1536]{1,0:T(8,128)(2,1)} %get-tuple-element.196), channel_id=1, source_target_pairs={{0,24},{1,25},{2,26},{3,27},{4,28},{5,29},{6,30},{7,31},{8,16},{9,... | collective-permute-start | bytes 884744 | tf_op jit(solution)/shard_map/ppermute | solution.py:109
  32.7 23.8 %collective-permute-start.4 = (bf16[4,96,768]{2,1,0:T(8,128)(2,1)}, bf16[4,96,768]{2,1,0:T(8,128)(2,1)}, u32[]{:S(2)}, u32[]{:S(2)}) collective-permute-start(bf16[4,96,768]{2,1,0:T(8,128)(2,1)} %pad_maximum_fusion.4.rest_0_.rest_8_), channel_id=1, source_target_pairs={{0,4},{1,3},{2,6},{3,1},{4,0},{5,7},{6,2},{7,5},{8,12},{9,11},{10,... | collective-permute-start | bytes 1769480 | tf_op jit(solution)/shard_map/ppermute | solution.py:109
  41.0 18.1 %collective-permute-start.6 = (bf16[4,96,768]{2,1,0:T(8,128)(2,1)}, bf16[4,96,768]{2,1,0:T(8,128)(2,1)S(1)}, u32[]{:S(2)}, u32[]{:S(2)}) collective-permute-start(bf16[4,96,768]{2,1,0:T(8,128)(2,1)} %pad_maximum_fusion.4.rest_0_.rest_8_), channel_id=1, source_target_pairs={{0,1},{1,0},{2,3},{3,2},{4,5},{5,4},{6,7},{7,6},{8,9},{9,8},{10,11... | collective-permute-start | bytes 1769480 | tf_op jit(solution)/shard_map/ppermute | solution.py:109
  41.0 16.0 %collective-permute-start.5 = (bf16[4,96,768]{2,1,0:T(8,128)(2,1)}, bf16[4,96,768]{2,1,0:T(8,128)(2,1)}, u32[]{:S(2)}, u32[]{:S(2)}) collective-permute-start(bf16[4,96,768]{2,1,0:T(8,128)(2,1)} %collective-permute-done.3.rest_1_.rest_9_), channel_id=1, source_target_pairs={{0,4},{1,3},{2,6},{3,1},{4,0},{5,7},{6,2},{7,5},{8,12},{9,11},{10,... | collective-permute-start | bytes 1769480 | tf_op jit(solution)/shard_map/ppermute | solution.py:109
  56.5 4.1 %collective-permute-start.7 = (bf16[4,96,768]{2,1,0:T(8,128)(2,1)}, bf16[4,96,768]{2,1,0:T(8,128)(2,1)}, u32[]{:S(2)}, u32[]{:S(2)}) collective-permute-start(bf16[4,96,768]{2,1,0:T(8,128)(2,1)} %collective-permute-done.3.rest_1_.rest_9_), channel_id=1, source_target_pairs={{0,1},{1,0},{2,3},{3,2},{4,5},{5,4},{6,7},{7,6},{8,9},{9,8},{10,11... | collective-permute-start | bytes 1769480 | tf_op jit(solution)/shard_map/ppermute | solution.py:109
  56.5 4.1 %collective-permute-start.8 = (bf16[4,96,768]{2,1,0:T(8,128)(2,1)}, bf16[4,96,768]{2,1,0:T(8,128)(2,1)}, u32[]{:S(2)}, u32[]{:S(2)}) collective-permute-start(bf16[4,96,768]{2,1,0:T(8,128)(2,1)} %collective-permute-done.4.rest_2_.rest_10_), channel_id=1, source_target_pairs={{0,1},{1,0},{2,3},{3,2},{4,5},{5,4},{6,7},{7,6},{8,9},{9,8},{10,11... | collective-permute-start | bytes 1769480 | tf_op jit(solution)/shard_map/ppermute | solution.py:109
  57.0 21.6 %collective-permute-start.13 = (bf16[4,96,768]{2,1,0:T(8,128)(2,1)}, bf16[4,96,768]{2,1,0:T(8,128)(2,1)}, u32[]{:S(2)}, u32[]{:S(2)}) collective-permute-start(bf16[4,96,768]{2,1,0:T(8,128)(2,1)} %get-tuple-element.70.rest_0_), channel_id=1, source_target_pairs={{0,2},{1,5},{2,0},{3,7},{4,6},{5,1},{6,4},{7,3},{8,10},{9,13},{10,... | collective-permute-start | bytes 1769480 | tf_op jit(solution)/shard_map/ppermute | solution.py:109
  57.5 21.1 %collective-permute-start.14 = (bf16[4,96,768]{2,1,0:T(8,128)(2,1)}, bf16[4,96,768]{2,1,0:T(8,128)(2,1)}, u32[]{:S(2)}, u32[]{:S(2)}) collective-permute-start(bf16[4,96,768]{2,1,0:T(8,128)(2,1)} %get-tuple-element.70.rest_0_), channel_id=1, source_target_pairs={{0,4},{1,3},{2,6},{3,1},{4,0},{5,7},{6,2},{7,5},{8,12},{9,11},{10,... | collective-permute-start | bytes 1769480 | tf_op jit(solution)/shard_map/ppermute | solution.py:109
  59.9 2.3 collective-permute-start.9
  78.6 28.9 %copy-start.9 = (f32[512,768]{1,0:T(8,128)}, f32[512,768]{1,0:T(8,128)S(1)}, u32[]{:S(2)}) copy-start(f32[512,768]{1,0:T(8,128)S(1)} %get-tuple-element.74.normed_ref) | copy-start | bytes 4718596
  78.6 10.2 %collective-permute-start.15 = (bf16[4,96,768]{2,1,0:T(8,128)(2,1)}, bf16[4,96,768]{2,1,0:T(8,128)(2,1)S(1)}, u32[]{:S(2)}, u32[]{:S(2)}) collective-permute-start(bf16[4,96,768]{2,1,0:T(8,128)(2,1)} %collective-permute-done.13.rest_1_), channel_id=1, source_target_pairs={{0,4},{1,3},{2,6},{3,1},{4,0},{5,7},{6,2},{7,5},{8,12},{9,11},{10,... | collective-permute-start | bytes 1769480 | tf_op jit(solution)/shard_map/ppermute | solution.py:109
  79.2 10.7 %collective-permute-start.16 = (bf16[4,96,768]{2,1,0:T(8,128)(2,1)}, bf16[4,96,768]{2,1,0:T(8,128)(2,1)S(1)}, u32[]{:S(2)}, u32[]{:S(2)}) collective-permute-start(bf16[4,96,768]{2,1,0:T(8,128)(2,1)} %get-tuple-element.70.rest_0_), channel_id=1, source_target_pairs={{0,1},{1,0},{2,3},{3,2},{4,5},{5,4},{6,7},{7,6},{8,9},{9,8},{10,11... | collective-permute-start | bytes 1769480 | tf_op jit(solution)/shard_map/ppermute | solution.py:109
  80.5 10.5 %collective-permute-start.17 = (bf16[4,96,768]{2,1,0:T(8,128)(2,1)}, bf16[4,96,768]{2,1,0:T(8,128)(2,1)S(1)}, u32[]{:S(2)}, u32[]{:S(2)}) collective-permute-start(bf16[4,96,768]{2,1,0:T(8,128)(2,1)} %collective-permute-done.13.rest_1_), channel_id=1, source_target_pairs={{0,1},{1,0},{2,3},{3,2},{4,5},{5,4},{6,7},{7,6},{8,9},{9,8},{10,11... | collective-permute-start | bytes 1769480 | tf_op jit(solution)/shard_map/ppermute | solution.py:109
  80.5 10.5 %collective-permute-start.18 = (bf16[4,96,768]{2,1,0:T(8,128)(2,1)}, bf16[4,96,768]{2,1,0:T(8,128)(2,1)S(1)}, u32[]{:S(2)}, u32[]{:S(2)}) collective-permute-start(bf16[4,96,768]{2,1,0:T(8,128)(2,1)} %collective-permute-done.14.rest_2_), channel_id=1, source_target_pairs={{0,1},{1,0},{2,3},{3,2},{4,5},{5,4},{6,7},{7,6},{8,9},{9,8},{10,11... | collective-permute-start | bytes 1769480 | tf_op jit(solution)/shard_map/ppermute | solution.py:109
  88.7 30.7 %copy-start.54 = (f32[768]{0:T(1024)S(1)}, f32[768]{0:T(1024)}, u32[]{:S(2)}) copy-start(f32[768]{0:T(1024)} %param.32) | copy-start | bytes 9220
  88.7 30.7 %copy-start.55 = (f32[768]{0:T(1024)S(1)}, f32[768]{0:T(1024)}, u32[]{:S(2)}) copy-start(f32[768]{0:T(1024)} %param.33) | copy-start | bytes 9220
  88.8 30.7 %copy-start.56 = (f32[768]{0:T(1024)S(1)}, f32[768]{0:T(1024)}, u32[]{:S(2)}) copy-start(f32[768]{0:T(1024)} %param.34) | copy-start | bytes 9220
  88.8 2.3 collective-permute-start.19
  88.9 20.3 %collective-permute-start.20 = (bf16[4,96,768]{2,1,0:T(8,128)(2,1)}, bf16[4,96,768]{2,1,0:T(8,128)(2,1)}, u32[]{:S(2)}, u32[]{:S(2)}) collective-permute-start(bf16[4,96,768]{2,1,0:T(8,128)(2,1)} %get-tuple-element.76.rest_0_), channel_id=1, source_target_pairs={{0,2},{1,5},{2,0},{3,7},{4,6},{5,1},{6,4},{7,3},{8,10},{9,13},{10,... | collective-permute-start | bytes 1769480 | tf_op jit(solution)/shard_map/ppermute | solution.py:109
  89.8 19.4 %collective-permute-start.21 = (bf16[4,96,768]{2,1,0:T(8,128)(2,1)}, bf16[4,96,768]{2,1,0:T(8,128)(2,1)}, u32[]{:S(2)}, u32[]{:S(2)}) collective-permute-start(bf16[4,96,768]{2,1,0:T(8,128)(2,1)} %get-tuple-element.76.rest_0_), channel_id=1, source_target_pairs={{0,4},{1,3},{2,6},{3,1},{4,0},{5,7},{6,2},{7,5},{8,12},{9,11},{10,... | collective-permute-start | bytes 1769480 | tf_op jit(solution)/shard_map/ppermute | solution.py:109
  109.2 10.2 %collective-permute-start.22 = (bf16[4,96,768]{2,1,0:T(8,128)(2,1)}, bf16[4,96,768]{2,1,0:T(8,128)(2,1)}, u32[]{:S(2)}, u32[]{:S(2)}) collective-permute-start(bf16[4,96,768]{2,1,0:T(8,128)(2,1)} %collective-permute-done.20.rest_1_), channel_id=1, source_target_pairs={{0,4},{1,3},{2,6},{3,1},{4,0},{5,7},{6,2},{7,5},{8,12},{9,11},{10,... | collective-permute-start | bytes 1769480 | tf_op jit(solution)/shard_map/ppermute | solution.py:109
  110.1 11.1 %collective-permute-start.24 = (bf16[4,96,768]{2,1,0:T(8,128)(2,1)}, bf16[4,96,768]{2,1,0:T(8,128)(2,1)}, u32[]{:S(2)}, u32[]{:S(2)}) collective-permute-start(bf16[4,96,768]{2,1,0:T(8,128)(2,1)} %collective-permute-done.20.rest_1_), channel_id=1, source_target_pairs={{0,1},{1,0},{2,3},{3,2},{4,5},{5,4},{6,7},{7,6},{8,9},{9,8},{10,11... | collective-permute-start | bytes 1769480 | tf_op jit(solution)/shard_map/ppermute | solution.py:109
  110.1 11.1 %collective-permute-start.23 = (bf16[4,96,768]{2,1,0:T(8,128)(2,1)}, bf16[4,96,768]{2,1,0:T(8,128)(2,1)}, u32[]{:S(2)}, u32[]{:S(2)}) collective-permute-start(bf16[4,96,768]{2,1,0:T(8,128)(2,1)} %get-tuple-element.76.rest_0_), channel_id=1, source_target_pairs={{0,1},{1,0},{2,3},{3,2},{4,5},{5,4},{6,7},{7,6},{8,9},{9,8},{10,11... | collective-permute-start | bytes 1769480 | tf_op jit(solution)/shard_map/ppermute | solution.py:109
  110.6 10.6 %collective-permute-start.25 = (bf16[4,96,768]{2,1,0:T(8,128)(2,1)}, bf16[4,96,768]{2,1,0:T(8,128)(2,1)}, u32[]{:S(2)}, u32[]{:S(2)}) collective-permute-start(bf16[4,96,768]{2,1,0:T(8,128)(2,1)} %collective-permute-done.21.rest_2_), channel_id=1, source_target_pairs={{0,1},{1,0},{2,3},{3,2},{4,5},{5,4},{6,7},{7,6},{8,9},{9,8},{10,11... | collective-permute-start | bytes 1769480 | tf_op jit(solution)/shard_map/ppermute | solution.py:109
  119.4 2.3 collective-permute-start.26
  136.6 13.3 %collective-permute-start.30 = (bf16[4,4,96,768]{3,2,1,0:T(8,128)(2,1)S(1)}, bf16[4,4,96,768]{3,2,1,0:T(8,128)(2,1)S(1)}, u32[]{:S(2)}, u32[]{:S(2)}) collective-permute-start(bf16[4,4,96,768]{3,2,1,0:T(8,128)(2,1)S(1)} %shard_map.309), channel_id=1, source_target_pairs={{0,1},{1,0},{2,3},{3,2},{4,5},{5,4},{6,7},{7,6},{8,9},{9,8},{10,11... | collective-permute-start | bytes 7077896 | tf_op jit(solution)/shard_map/ppermute | solution.py:109
  143.5 39.8 %copy-start.4 = (bf16[4,4,96,768]{3,2,1,0:T(8,128)(2,1)}, bf16[4,4,96,768]{3,2,1,0:T(8,128)(2,1)S(1)}, u32[]{:S(2)}) copy-start(bf16[4,4,96,768]{3,2,1,0:T(8,128)(2,1)S(1)} %shard_map.310) | copy-start | bytes 7077892
  149.9 33.3 %copy-start.46 = (bf16[4,4,96,768]{3,2,1,0:T(8,128)(2,1)}, bf16[4,4,96,768]{3,2,1,0:T(8,128)(2,1)S(1)}, u32[]{:S(2)}) copy-start(bf16[4,4,96,768]{3,2,1,0:T(8,128)(2,1)S(1)} %collective-permute-done.30) | copy-start | bytes 7077892
  157.8 26.6 %collective-permute-start.31 = (bf16[4,4,96,768]{3,2,1,0:T(8,128)(2,1)S(1)}, bf16[4,4,96,768]{3,2,1,0:T(8,128)(2,1)S(1)}, u32[]{:S(2)}, u32[]{:S(2)}) collective-permute-start(bf16[4,4,96,768]{3,2,1,0:T(8,128)(2,1)S(1)} %shard_map.312), channel_id=1, source_target_pairs={{0,1},{1,0},{2,3},{3,2},{4,5},{5,4},{6,7},{7,6},{8,9},{9,8},{10,11... | collective-permute-start | bytes 7077896 | tf_op jit(solution)/shard_map/ppermute | solution.py:109
  158.6 24.6 %collective-permute-start.32 = (bf16[2,4,96,768]{3,2,1,0:T(8,128)(2,1)S(1)}, bf16[2,4,96,768]{3,2,1,0:T(8,128)(2,1)S(1)}, u32[]{:S(2)}, u32[]{:S(2)}) collective-permute-start(bf16[2,4,96,768]{3,2,1,0:T(8,128)(2,1)S(1)} %pad_maximum_fusion.1), channel_id=1, source_target_pairs={{0,2},{1,5},{2,0},{3,7},{4,6},{5,1},{6,4},{7,3},{8,10},{9,13},{10,... | collective-permute-start | bytes 3538952 | tf_op jit(solution)/shard_map/ppermute | solution.py:109
  159.6 46.8 %collective-permute-start.27 = (bf16[512,768]{1,0:T(8,128)(2,1)}, bf16[512,768]{1,0:T(8,128)(2,1)}, u32[]{:S(2)}, u32[]{:S(2)}) collective-permute-start(bf16[512,768]{1,0:T(8,128)(2,1)} %get-tuple-element.79.one), channel_id=1, source_target_pairs={{0,2},{1,3},{2,0},{3,1},{4,6},{5,7},{6,4},{7,5},{8,10},{9,11},{10,... | collective-permute-start | bytes 2359304 | tf_op jit(solution)/shard_map/ppermute | solution.py:109
  205.9 41.9 %collective-permute-start.34 = (bf16[4,4,96,768]{3,2,1,0:T(8,128)(2,1)}, bf16[4,4,96,768]{3,2,1,0:T(8,128)(2,1)}, u32[]{:S(2)}, u32[]{:S(2)}) collective-permute-start(bf16[4,4,96,768]{3,2,1,0:T(8,128)(2,1)} %get-tuple-element.104), channel_id=1, source_target_pairs={{0,1},{1,0},{2,3},{3,2},{4,5},{5,4},{6,7},{7,6},{8,9},{9,8},{10,11... | collective-permute-start | bytes 7077896 | tf_op jit(solution)/shard_map/ppermute | solution.py:109
  205.9 6.0 %collective-permute-start.28 = (bf16[512,768]{1,0:T(8,128)(2,1)}, bf16[512,768]{1,0:T(8,128)(2,1)}, u32[]{:S(2)}, u32[]{:S(2)}) collective-permute-start(bf16[512,768]{1,0:T(8,128)(2,1)} %get-tuple-element.79.one), channel_id=1, source_target_pairs={{0,1},{1,0},{2,3},{3,2},{4,5},{5,4},{6,7},{7,6},{8,9},{9,8},{10,11... | collective-permute-start | bytes 2359304 | tf_op jit(solution)/shard_map/ppermute | solution.py:109
  206.4 6.6 %collective-permute-start.29 = (bf16[512,768]{1,0:T(8,128)(2,1)}, bf16[512,768]{1,0:T(8,128)(2,1)}, u32[]{:S(2)}, u32[]{:S(2)}) collective-permute-start(bf16[512,768]{1,0:T(8,128)(2,1)} %collective-permute-done.27.two), channel_id=1, source_target_pairs={{0,1},{1,0},{2,3},{3,2},{4,5},{5,4},{6,7},{7,6},{8,9},{9,8},{10,11... | collective-permute-start | bytes 2359304 | tf_op jit(solution)/shard_map/ppermute | solution.py:109
  206.4 16.3 %collective-permute-start.53 = (bf16[4,96,768]{2,1,0:T(8,128)(2,1)}, bf16[4,96,768]{2,1,0:T(8,128)(2,1)}, u32[]{:S(2)}, u32[]{:S(2)}) collective-permute-start(bf16[4,96,768]{2,1,0:T(8,128)(2,1)} %fusion), channel_id=1, source_target_pairs={{0,4},{1,3},{2,6},{3,1},{4,0},{5,7},{6,2},{7,5},{8,12},{9,11},{10,... | collective-permute-start | bytes 1769480 | tf_op jit(solution)/shard_map/ppermute | solution.py:109
  207.3 29.9 %collective-permute-start.33 = (bf16[2,4,96,768]{3,2,1,0:T(8,128)(2,1)}, bf16[2,4,96,768]{3,2,1,0:T(8,128)(2,1)}, u32[]{:S(2)}, u32[]{:S(2)}) collective-permute-start(bf16[2,4,96,768]{3,2,1,0:T(8,128)(2,1)} %pad_maximum_fusion.2), channel_id=1, source_target_pairs={{0,2},{1,5},{2,0},{3,7},{4,6},{5,1},{6,4},{7,3},{8,10},{9,13},{10,... | collective-permute-start | bytes 3538952 | tf_op jit(solution)/shard_map/ppermute | solution.py:109
  211.9 10.8 %collective-permute-start.43 = (f32[80,128]{1,0:T(8,128)S(1)}, f32[80,128]{1,0:T(8,128)S(1)}, u32[]{:S(2)}, u32[]{:S(2)}) collective-permute-start(f32[80,128]{1,0:T(8,128)S(1)} %maximum_bitcast_fusion.1), channel_id=1, source_target_pairs={{0,1},{1,0},{2,3},{3,2},{4,5},{5,4},{6,7},{7,6},{8,9},{9,8},{10,11... | collective-permute-start | bytes 122888 | tf_op jit(solution)/shard_map/ppermute | solution.py:109
  222.7 6.4 %collective-permute-start.44 = (f32[80,128]{1,0:T(8,128)S(1)}, f32[80,128]{1,0:T(8,128)S(1)}, u32[]{:S(2)}, u32[]{:S(2)}) collective-permute-start(f32[80,128]{1,0:T(8,128)S(1)} %fusion.22), channel_id=1, source_target_pairs={{0,2},{1,5},{2,0},{3,7},{4,6},{5,1},{6,4},{7,3},{8,10},{9,13},{10,... | collective-permute-start | bytes 122888 | tf_op jit(solution)/shard_map/ppermute | solution.py:109
  229.1 6.7 %collective-permute-start.45 = (f32[80,128]{1,0:T(8,128)S(1)}, f32[80,128]{1,0:T(8,128)S(1)}, u32[]{:S(2)}, u32[]{:S(2)}) collective-permute-start(f32[80,128]{1,0:T(8,128)S(1)} %fusion.24), channel_id=1, source_target_pairs={{0,4},{1,3},{2,6},{3,1},{4,0},{5,7},{6,2},{7,5},{8,12},{9,11},{10,... | collective-permute-start | bytes 122888 | tf_op jit(solution)/shard_map/ppermute | solution.py:109
  230.1 20.6 %collective-permute-start.54 = (bf16[96,768]{1,0:T(8,128)(2,1)S(1)}, bf16[96,768]{1,0:T(8,128)(2,1)S(1)}, u32[]{:S(2)}, u32[]{:S(2)}) collective-permute-start(bf16[96,768]{1,0:T(8,128)(2,1)S(1)} %get-tuple-element.178), channel_id=1, source_target_pairs={{0,8},{1,9},{2,10},{3,11},{4,12},{5,13},{6,14},{7,15},{8,0},{9,1},... | collective-permute-start | bytes 442376 | tf_op jit(solution)/shard_map/ppermute | solution.py:109
  234.6 17.6 %collective-permute-start.55 = (bf16[96,768]{1,0:T(8,128)(2,1)S(1)}, bf16[96,768]{1,0:T(8,128)(2,1)S(1)}, u32[]{:S(2)}, u32[]{:S(2)}) collective-permute-start(bf16[96,768]{1,0:T(8,128)(2,1)S(1)} %get-tuple-element.180), channel_id=1, source_target_pairs={{0,16},{1,17},{2,18},{3,19},{4,20},{5,21},{6,22},{7,23},{8,24},{9,... | collective-permute-start | bytes 442376 | tf_op jit(solution)/shard_map/ppermute | solution.py:109
  235.8 17.7 %collective-permute-start.56 = (bf16[96,768]{1,0:T(8,128)(2,1)S(1)}, bf16[96,768]{1,0:T(8,128)(2,1)S(1)}, u32[]{:S(2)}, u32[]{:S(2)}) collective-permute-start(bf16[96,768]{1,0:T(8,128)(2,1)S(1)} %get-tuple-element.179), channel_id=1, source_target_pairs={{0,24},{1,25},{2,26},{3,27},{4,28},{5,29},{6,30},{7,31},{8,16},{9,... | collective-permute-start | bytes 442376 | tf_op jit(solution)/shard_map/ppermute | solution.py:109
  237.2 17.1 %collective-permute-start.46 = (f32[80,128]{1,0:T(8,128)S(1)}, f32[80,128]{1,0:T(8,128)S(1)}, u32[]{:S(2)}, u32[]{:S(2)}) collective-permute-start(f32[80,128]{1,0:T(8,128)S(1)} %add.230), channel_id=1, source_target_pairs={{0,8},{1,9},{2,10},{3,11},{4,12},{5,13},{6,14},{7,15},{8,0},{9,1},... | collective-permute-start | bytes 122888 | tf_op jit(solution)/shard_map/ppermute | solution.py:109
  247.8 6.6 %collective-permute-start.47 = (f32[80,128]{1,0:T(8,128)S(1)}, f32[80,128]{1,0:T(8,128)S(1)}, u32[]{:S(2)}, u32[]{:S(2)}) collective-permute-start(f32[80,128]{1,0:T(8,128)S(1)} %add.230), channel_id=1, source_target_pairs={{0,16},{1,17},{2,18},{3,19},{4,20},{5,21},{6,22},{7,23},{8,24},{9,... | collective-permute-start | bytes 122888 | tf_op jit(solution)/shard_map/ppermute | solution.py:109
  250.7 5.9 %collective-permute-start.48 = (f32[80,128]{1,0:T(8,128)S(1)}, f32[80,128]{1,0:T(8,128)S(1)}, u32[]{:S(2)}, u32[]{:S(2)}) collective-permute-start(f32[80,128]{1,0:T(8,128)S(1)} %add.230), channel_id=1, source_target_pairs={{0,24},{1,25},{2,26},{3,27},{4,28},{5,29},{6,30},{7,31},{8,16},{9,... | collective-permute-start | bytes 122888 | tf_op jit(solution)/shard_map/ppermute | solution.py:109
  252.2 22.5 %collective-permute-start.35 = (bf16[2,4,96,768]{3,2,1,0:T(8,128)(2,1)S(1)}, bf16[2,4,96,768]{3,2,1,0:T(8,128)(2,1)S(1)}, u32[]{:S(2)}, u32[]{:S(2)}) collective-permute-start(bf16[2,4,96,768]{3,2,1,0:T(8,128)(2,1)S(1)} %pad_maximum_fusion.3), channel_id=1, source_target_pairs={{0,2},{1,5},{2,0},{3,7},{4,6},{5,1},{6,4},{7,3},{8,10},{9,13},{10,... | collective-permute-start | bytes 3538952 | tf_op jit(solution)/shard_map/ppermute | solution.py:109
  257.3 21.0 %collective-permute-start.49 = (bf16[4,96,768]{2,1,0:T(8,128)(2,1)S(1)}, bf16[4,96,768]{2,1,0:T(8,128)(2,1)S(1)}, u32[]{:S(2)}, u32[]{:S(2)}) collective-permute-start(bf16[4,96,768]{2,1,0:T(8,128)(2,1)S(1)} %fusion.1), channel_id=1, source_target_pairs={{0,4},{1,3},{2,6},{3,1},{4,0},{5,7},{6,2},{7,5},{8,12},{9,11},{10,... | collective-permute-start | bytes 1769480 | tf_op jit(solution)/shard_map/ppermute | solution.py:109
  276.0 9.9 %collective-permute-start.39 = (bf16[4,96,768]{2,1,0:T(8,128)(2,1)S(1)}, bf16[4,96,768]{2,1,0:T(8,128)(2,1)S(1)}, u32[]{:S(2)}, u32[]{:S(2)}) collective-permute-start(bf16[4,96,768]{2,1,0:T(8,128)(2,1)S(1)} %fusion.2), channel_id=1, source_target_pairs={{0,4},{1,3},{2,6},{3,1},{4,0},{5,7},{6,2},{7,5},{8,12},{9,11},{10,... | collective-permute-start | bytes 1769480 | tf_op jit(solution)/shard_map/ppermute | solution.py:109
  279.7 8.6 %collective-permute-start.50 = (bf16[96,768]{1,0:T(8,128)(2,1)S(1)}, bf16[96,768]{1,0:T(8,128)(2,1)S(1)}, u32[]{:S(2)}, u32[]{:S(2)}) collective-permute-start(bf16[96,768]{1,0:T(8,128)(2,1)S(1)} %get-tuple-element.181), channel_id=1, source_target_pairs={{0,8},{1,9},{2,10},{3,11},{4,12},{5,13},{6,14},{7,15},{8,0},{9,1},... | collective-permute-start | bytes 442376 | tf_op jit(solution)/shard_map/ppermute | solution.py:109
  280.9 13.8 %collective-permute-start.51 = (bf16[96,768]{1,0:T(8,128)(2,1)S(1)}, bf16[96,768]{1,0:T(8,128)(2,1)S(1)}, u32[]{:S(2)}, u32[]{:S(2)}) collective-permute-start(bf16[96,768]{1,0:T(8,128)(2,1)S(1)} %get-tuple-element.183), channel_id=1, source_target_pairs={{0,16},{1,17},{2,18},{3,19},{4,20},{5,21},{6,22},{7,23},{8,24},{9,... | collective-permute-start | bytes 442376 | tf_op jit(solution)/shard_map/ppermute | solution.py:109
  282.6 13.6 %collective-permute-start.52 = (bf16[96,768]{1,0:T(8,128)(2,1)S(1)}, bf16[96,768]{1,0:T(8,128)(2,1)S(1)}, u32[]{:S(2)}, u32[]{:S(2)}) collective-permute-start(bf16[96,768]{1,0:T(8,128)(2,1)S(1)} %get-tuple-element.182), channel_id=1, source_target_pairs={{0,24},{1,25},{2,26},{3,27},{4,28},{5,29},{6,30},{7,31},{8,16},{9,... | collective-permute-start | bytes 442376 | tf_op jit(solution)/shard_map/ppermute | solution.py:109
  284.2 21.8 %collective-permute-start.36 = (bf16[512,768]{1,0:T(8,128)(2,1)}, bf16[512,768]{1,0:T(8,128)(2,1)S(1)}, u32[]{:S(2)}, u32[]{:S(2)}) collective-permute-start(bf16[512,768]{1,0:T(8,128)(2,1)} %shard_map.317.one), channel_id=1, source_target_pairs={{0,2},{1,3},{2,0},{3,1},{4,6},{5,7},{6,4},{7,5},{8,10},{9,11},{10,... | collective-permute-start | bytes 2359304 | tf_op jit(solution)/shard_map/ppermute | solution.py:109
  287.4 9.7 %collective-permute-start.40 = (bf16[96,768]{1,0:T(8,128)(2,1)S(1)}, bf16[96,768]{1,0:T(8,128)(2,1)S(1)}, u32[]{:S(2)}, u32[]{:S(2)}) collective-permute-start(bf16[96,768]{1,0:T(8,128)(2,1)S(1)} %get-tuple-element.184), channel_id=1, source_target_pairs={{0,8},{1,9},{2,10},{3,11},{4,12},{5,13},{6,14},{7,15},{8,0},{9,1},... | collective-permute-start | bytes 442376 | tf_op jit(solution)/shard_map/ppermute | solution.py:109
  288.3 17.5 %collective-permute-start.41 = (bf16[96,768]{1,0:T(8,128)(2,1)S(1)}, bf16[96,768]{1,0:T(8,128)(2,1)S(1)}, u32[]{:S(2)}, u32[]{:S(2)}) collective-permute-start(bf16[96,768]{1,0:T(8,128)(2,1)S(1)} %get-tuple-element.186), channel_id=1, source_target_pairs={{0,16},{1,17},{2,18},{3,19},{4,20},{5,21},{6,22},{7,23},{8,24},{9,... | collective-permute-start | bytes 442376 | tf_op jit(solution)/shard_map/ppermute | solution.py:109
  294.7 11.2 %collective-permute-start.42 = (bf16[96,768]{1,0:T(8,128)(2,1)S(1)}, bf16[96,768]{1,0:T(8,128)(2,1)S(1)}, u32[]{:S(2)}, u32[]{:S(2)}) collective-permute-start(bf16[96,768]{1,0:T(8,128)(2,1)S(1)} %get-tuple-element.185), channel_id=1, source_target_pairs={{0,24},{1,25},{2,26},{3,27},{4,28},{5,29},{6,30},{7,31},{8,16},{9,... | collective-permute-start | bytes 442376 | tf_op jit(solution)/shard_map/ppermute | solution.py:109
  297.1 12.7 %collective-permute-start.37 = (bf16[512,768]{1,0:T(8,128)(2,1)}, bf16[512,768]{1,0:T(8,128)(2,1)S(1)}, u32[]{:S(2)}, u32[]{:S(2)}) collective-permute-start(bf16[512,768]{1,0:T(8,128)(2,1)} %shard_map.317.one), channel_id=1, source_target_pairs={{0,1},{1,0},{2,3},{3,2},{4,5},{5,4},{6,7},{7,6},{8,9},{9,8},{10,11... | collective-permute-start | bytes 2359304 | tf_op jit(solution)/shard_map/ppermute | solution.py:109
  306.0 4.7 %collective-permute-start.38 = (bf16[512,768]{1,0:T(8,128)(2,1)S(1)}, bf16[512,768]{1,0:T(8,128)(2,1)S(1)}, u32[]{:S(2)}, u32[]{:S(2)}) collective-permute-start(bf16[512,768]{1,0:T(8,128)(2,1)S(1)} %collective-permute-done.36.two), channel_id=1, source_target_pairs={{0,1},{1,0},{2,3},{3,2},{4,5},{5,4},{6,7},{7,6},{8,9},{9,8},{10,11... | collective-permute-start | bytes 2359304 | tf_op jit(solution)/shard_map/ppermute | solution.py:109
  (51 other events, 352.0 us)
